TPU v7x, 256 devices: a whole 4x4x8 slice. The times are simulated.
256 devices in a mesh: head: 4 (over y_hi, core), blk: 64 (over z, x, y_lo).
Axes of the slice: x: 4, y: 4 (y_hi: 2, y_lo: 2; y = y_hi * 2 + y_lo), z: 8, core: 2. Of those that a mesh axis runs over, the one named last changes fastest.
Arguments:
- queries: bfloat16 [32768, 5120], P(('head', 'blk')), may hold values from -120 to 120
- keys: bfloat16 [32768, 5120], P(('head', 'blk')), may hold values from -120 to 120
- values: bfloat16 [32768, 5120], P(('head', 'blk')), may hold values from -6 to 6
- queries_tan: bfloat16 [32768, 5120], P(('head', 'blk')), may hold values from -6 to 6
- keys_tan: bfloat16 [32768, 5120], P(('head', 'blk')), may hold values from -6 to 6
- values_tan: bfloat16 [32768, 5120], P(('head', 'blk')), may hold values from -6 to 6
Outputs:
- attended: bfloat16 [32768, 5120], P(('head', 'blk'))
- attended_tan: bfloat16 [32768, 5120], P(('head', 'blk'))
- log_total: float32 [32768, 40], P(('head', 'blk'))
- log_total_tan: float32 [32768, 40], P(('head', 'blk'))
All inputs are finite; a program needn't handle non-finite values.
Results may differ from a plain program's by a relative error of at most 0.005.
Values may be sent and summed in bfloat16 or wider, within the bound.
No kernel may reach another device: no remote copies, remote signals or barrier semaphores. Data moves between devices by JAX's collectives and lax.ppermute only.
A program may use at most 128 MiB of HBM per device.

v0:
```python
import jax
import jax.numpy as jnp
from jax import lax
from jax.sharding import PartitionSpec as P

DH = 128


def shifted(value, axis, by):
    length = lax.axis_size(axis)
    return lax.ppermute(value, axis, [(i, (i + by) % length) for i in range(length)])


def one_head(pieces):
    query_rows, query_tan, key_rows, key_tan, value_rows, value_tan = pieces
    score_scale = 1.0 / DH**0.5
    scores = (
        jnp.einsum("td,kd->tk", query_rows, key_rows, preferred_element_type=jnp.float32)
        * score_scale
    )
    joined_q = jnp.concatenate([query_tan, query_rows], axis=-1)
    joined_k = jnp.concatenate([key_rows, key_tan], axis=-1)
    tangent_scores = (
        jnp.einsum("td,kd->tk", joined_q, joined_k, preferred_element_type=jnp.float32)
        * score_scale
    )
    row_max = jnp.max(scores, axis=-1, keepdims=True)
    expo = jnp.exp(scores - row_max)
    row_sum = jnp.sum(expo, axis=-1, keepdims=True)
    probs = expo / row_sum
    log_total = (row_max + jnp.log(row_sum))[:, 0]
    log_total_tan = jnp.sum(probs * tangent_scores, axis=-1)
    probs_tan = probs * (tangent_scores - log_total_tan[:, None])
    probs_low = probs.astype(jnp.bfloat16)
    probs_tan_low = probs_tan.astype(jnp.bfloat16)
    attended = jnp.dot(probs_low, value_rows, preferred_element_type=jnp.float32)
    joined_p = jnp.concatenate([probs_tan_low, probs_low], axis=-1)
    joined_v = jnp.concatenate([value_rows, value_tan], axis=0)
    attended_tan = jnp.dot(joined_p, joined_v, preferred_element_type=jnp.float32)
    return (attended, attended_tan, log_total, log_total_tan)


def attend(paired, keyset):
    tokens_here = paired.shape[0]
    heads_here = paired.shape[2] // DH

    def heads_first(matrix):
        return matrix.reshape(matrix.shape[0], heads_here, DH).transpose(1, 0, 2)

    pieces = (
        heads_first(paired[:, 0]),
        heads_first(paired[:, 1]),
        heads_first(keyset[:, 0]),
        heads_first(keyset[:, 2]),
        heads_first(keyset[:, 1]),
        heads_first(keyset[:, 3]),
    )
    attended, attended_tan, log_total, log_total_tan = lax.map(one_head, pieces)
    attended = attended.transpose(1, 0, 2).reshape(tokens_here, -1)
    attended_tan = attended_tan.transpose(1, 0, 2).reshape(tokens_here, -1)
    outputs = jnp.stack([attended, attended_tan], axis=1).astype(jnp.bfloat16)
    statistics = jnp.stack([log_total.T, log_total_tan.T], axis=1)
    return (outputs, statistics)


def per_device(queries, keys, values, queries_tan, keys_tan, values_tan):
    bundle = jnp.stack([queries, queries_tan, keys, values, keys_tan, values_tan], axis=1)
    local_rows = lax.all_to_all(bundle, "head", split_axis=2, concat_axis=0, tiled=True)
    paired = local_rows[:, 0:2]
    key_stack = local_rows[:, 2:6]
    from_before = shifted(key_stack, "blk", 1)
    from_after = shifted(key_stack, "blk", -1)
    keyset = jnp.concatenate([from_before, key_stack, from_after], axis=0)
    outputs, statistics = attend(paired, keyset)
    back_rows = lax.all_to_all(outputs, "head", split_axis=0, concat_axis=2, tiled=True)
    back_stats = lax.all_to_all(statistics, "head", split_axis=0, concat_axis=2, tiled=True)
    return (back_rows[:, 0], back_rows[:, 1], back_stats[:, 0], back_stats[:, 1])


def solution(mesh):
    placed = (
        P(("head", "blk"), None),
        P(("head", "blk"), None),
        P(("head", "blk"), None),
        P(("head", "blk"), None),
        P(("head", "blk"), None),
        P(("head", "blk"), None),
    )
    return jax.shard_map(
        per_device,
        mesh=mesh,
        in_specs=placed,
        out_specs=(
            P(("head", "blk"), None),
            P(("head", "blk"), None),
            P(("head", "blk"), None),
            P(("head", "blk"), None),
        ),
        check_vma=False,
    )
```

profile of v0, /device:TPU:1, one launch (start us, length us, event | category | flops | bytes accessed | tf_op | source)
XLA Modules:
  0.0 762.7 jit_solution(7560107927044731392)
XLA Ops:
  0.7 2.6 bitcast_dynamic-update-slice_fusion.5
  9.1 13.8 %copy.112 = bf16[128,6,5120]{0,1,2:T(8,128)(2,1)} copy(bf16[128,6,5120]{2,0,1:T(8,128)(2,1)} %bitcast_dynamic-update-slice_fusion) | data formatting | bytes 15728640 | tf_op jit(solution)/shard_map/stack | solution.py:67
  22.9 127.8 %all_to_all.54 = bf16[128,6,5120]{0,1,2:T(8,128)(2,1)} all-to-all(bf16[128,6,5120]{0,1,2:T(8,128)(2,1)} %copy.112), channel_id=1, replica_groups=mesh['head'=4,'blk'=64] {'head'}, dimensions={2} | all-to-all | bytes 15728640 | tf_op jit(solution)/shard_map/all_to_all | solution.py:68
  150.7 15.1 %copy.114 = bf16[4,128,6,1280]{3,1,0,2:T(8,128)(2,1)} copy(bf16[4,128,6,1280]{1,2,3,0:T(8,128)(2,1)} %bitcast.119) | data formatting | bytes 15728640 | tf_op jit(solution)/shard_map/all_to_all | solution.py:68
  165.8 5.2 slice.48
  171.0 7.0 collective-permute-start.1
  183.0 214.2 %collective-permute-done.1 = bf16[512,4,1280]{2,0,1:T(8,128)(2,1)} collective-permute-done((bf16[512,4,1280]{2,0,1:T(8,128)(2,1)}, bf16[512,4,1280]{2,0,1:T(8,128)(2,1)}, u32[]{:S(2)}, u32[]{:S(2)}) %collective-permute-start.1) | collective-permute-done | bytes 5242912 | tf_op jit(solution)/shard_map/ppermute | solution.py:11
  397.2 7.6 pad_maximum_fusion
  404.8 5.6 fusion.29
  410.4 6.3 copy.116
  416.7 6.3 copy.117
  423.0 6.2 copy.119
  429.2 6.3 copy.120
  435.5 264.5 %while.16 = (s32[]{:T(128)}, bf16[10,512,128]{1,2,0:T(8,128)(2,1)}, bf16[10,512,128]{1,2,0:T(8,128)(2,1)}, f32[10,512]{1,0:T(8,128)}, f32[10,512]{1,0:T(8,128)},...) while((s32[]{:T(128)}, bf16[10,512,128]{1,2,0:T(8,128)(2,1)}, ...), condition=%wide.region_4.5_spmd, body=%wide.region_0.4_spmd.sunk | while | flops 1229716480 | bytes 53642536 | solution.py:58
  453.3 2.3 fusion.47
  456.0 3.2 fusion.48
  479.7 2.3 fusion.47
  482.5 3.2 fusion.48
  508.9 3.2 fusion.48
  535.4 3.2 fusion.48
  561.8 3.2 fusion.48
  588.3 3.2 fusion.48
  614.7 3.2 fusion.48
  641.2 3.2 fusion.48
  667.6 3.2 fusion.48
  694.1 3.2 fusion.48
  703.3 5.2 all-to-all-start.2
  710.4 4.8 copy.129
  715.3 4.8 all-to-all-start.1
  723.0 29.0 %all-to-all-done.1 = bf16[512,2,1280]{2,1,0:T(2,128)(2,1)S(1)} async-done(((bf16[512,2,1280]{2,1,0:T(2,128)(2,1)}), bf16[512,2,1280]{2,1,0:T(2,128)(2,1)S(1)}, u32[]{:S(2)}, u32[]{:S(2)}) %all-to-all-start.1) | async-done | bytes 2621472 | tf_op jit(solution)/shard_map/all_to_all | solution.py:75
  753.8 3.2 copy.131
  758.7 2.5 copy.135
  (310 shorter events, 250.7 us)
Async XLA Ops:
  0.6 3.9 copy-start.7
  171.0 226.2 %collective-permute-start.1 = (bf16[512,4,1280]{2,0,1:T(8,128)(2,1)}, bf16[512,4,1280]{2,0,1:T(8,128)(2,1)}, u32[]{:S(2)}, u32[]{:S(2)}) collective-permute-start(bf16[512,4,1280]{2,0,1:T(8,128)(2,1)} %slice.48), channel_id=1, source_target_pairs={{0,63},{1,0},{2,1},{3,2},{4,3},{5,4},{6,5},{7,6},{8,7},{9,8},{10,9... | collective-permute-start | bytes 15728648 | tf_op jit(solution)/shard_map/ppermute | solution.py:11
  178.1 219.1 %collective-permute-start = (bf16[512,4,1280]{2,0,1:T(8,128)(2,1)}, bf16[512,4,1280]{2,0,1:T(8,128)(2,1)}, u32[]{:S(2)}, u32[]{:S(2)}) collective-permute-start(bf16[512,4,1280]{2,0,1:T(8,128)(2,1)} %slice.48), channel_id=1, source_target_pairs={{0,1},{1,2},{2,3},{3,4},{4,5},{5,6},{6,7},{7,8},{8,9},{9,10},{10,1... | collective-permute-start | bytes 15728648 | tf_op jit(solution)/shard_map/ppermute | solution.py:11
  450.1 5.5 copy-start.3
  452.1 3.7 copy-start.2
  452.1 3.9 copy-start.1
  476.5 5.5 copy-start.3
  478.6 3.7 copy-start.2
  478.6 3.9 copy-start.1
  503.0 5.5 copy-start.3
  505.0 3.9 copy-start.1
  529.4 5.5 copy-start.3
  531.5 3.7 copy-start.2
  531.5 3.9 copy-start.1
  555.9 5.5 copy-start.3
  557.9 3.7 copy-start.2
  557.9 3.9 copy-start.1
  582.3 5.5 copy-start.3
  584.4 3.9 copy-start.1
  608.8 5.5 copy-start.3
  610.8 3.7 copy-start.2
  610.8 3.9 copy-start.1
  635.2 5.5 copy-start.3
  637.3 3.7 copy-start.2
  637.3 3.9 copy-start.1
  661.7 5.5 copy-start.3
  663.7 3.7 copy-start.2
  663.7 3.9 copy-start.1
  688.2 5.5 copy-start.3
  690.2 3.9 copy-start.1
  703.3 12.0 %all-to-all-start.2 = ((f32[4,1,2560]{2,1,0:T(1,128)}), f32[4,1,2560]{2,1,0:T(1,128)S(1)}, u32[]{:S(2)}, u32[]{:S(2)}) async-start(f32[4,1,2560]{2,1,0:T(1,128)} %reshape.32), calls=%async_computation.2 | async-start | bytes 81920 | tf_op jit(solution)/shard_map/all_to_all | solution.py:76
  715.3 36.8 %all-to-all-start.1 = ((bf16[512,2,1280]{2,1,0:T(2,128)(2,1)}), bf16[512,2,1280]{2,1,0:T(2,128)(2,1)S(1)}, u32[]{:S(2)}, u32[]{:S(2)}) async-start(bf16[512,2,1280]{2,1,0:T(2,128)(2,1)} %copy.129), calls=%async_computation.1 | async-start | bytes 5242880 | tf_op jit(solution)/shard_map/all_to_all | solution.py:75
  (28 other events, 41.5 us)
where the time goes:
time: 768 us; the launch traced here: 763 us
  local copies, waits for them, and re-layouts  253 us (33%)
  waiting for transfers between devices  243 us (32%)
  blocking collectives  128 us (17%)
  matrix products  83.8 us (11%)
  other arithmetic  36.1 us (5%)
  starting transfers between devices  17 us (2%)
    ppermute x2, waiting for transfers between devices, shifted(): lax.ppermute(value, axis, [(i, (i + by) % length) for i in range(length)])  214 us
    all_to_all x1, blocking collectives, per_device(): lax.all_to_all(bundle, 'head', split_axis=2, concat_axis=0, tiled=True)  128 us
    dynamic_slice x90, local copies, waits for them, and re-layouts, attend(): attended, attended_tan, log_total, log_total_tan = lax.map(one_head, pieces)  109 us
    dot_general x10, matrix products, one_head(): jnp.dot(joined_p, joined_v, preferred_element_type=jnp.float32)  32.4 us
    all_to_all x1, waiting for transfers between devices, per_device(): lax.all_to_all(outputs, 'head', split_axis=0, concat_axis=2, tiled=True)  29 us
    dynamic_update_slice x20, local copies, waits for them, and re-layouts, attend(): attended, attended_tan, log_total, log_total_tan = lax.map(one_head, pieces)  26.7 us
    dot_general x10, matrix products, one_head(): jnp.dot(probs_low, value_rows, preferred_element_type=jnp.float32)  22.9 us
    dot_general x10, matrix products, one_head(): jnp.einsum('td,kd->tk', joined_q, joined_k, preferred_element_type=jnp.fl...  21.7 us
  transfers between devices with their start and end apart: 4, of which 2 were waited for; matrix products, arithmetic and copies ran while one was open for 2% of the time, Pallas kernels for 0%

commit v1 on v0

v1 whole, which is shorter than its diff:
```python
import functools

import jax
import jax.numpy as jnp
from jax import lax
from jax.experimental import pallas as pl
from jax.experimental.pallas import tpu as pltpu
from jax.sharding import Mesh, PartitionSpec as P

DH = 128
SEG = 128
GROUP = 8
BLK = 512
ROWS = 256
OUT_ROWS = 2 * SEG + 16
SCALE = 1.0 / DH**0.5
LOG2E = 1.4426950408889634
AXES = ("y_hi", "core", "z", "x", "y_lo")
RING = ("y_lo", "y_hi", "core")
LINE = ("z", "x")
CHUNKS = (2, 2, 1)


def pack(arrays, base, nh):
    width = nh * DH

    def body(q, k, v, dq, dk, dv, q_out, kv_out):
        for j in range(nh):
            cols = pl.ds(j * DH, DH)
            q_out[:, pl.ds((2 * j) * DH, DH)] = dq[:, cols]
            q_out[:, pl.ds((2 * j + 1) * DH, DH)] = q[:, cols]
            kv_out[:, pl.ds((4 * j) * DH, DH)] = k[:, cols]
            kv_out[:, pl.ds((4 * j + 1) * DH, DH)] = dk[:, cols]
            kv_out[:, pl.ds((4 * j + 2) * DH, DH)] = v[:, cols]
            kv_out[:, pl.ds((4 * j + 3) * DH, DH)] = dv[:, cols]

    first = base // nh
    spec = pl.BlockSpec((SEG, width), lambda d: (0, first + d))
    return pl.pallas_call(
        body,
        grid=(GROUP,),
        in_specs=[spec] * 6,
        out_specs=[
            pl.BlockSpec((SEG, 2 * width), lambda d: (d, 0)),
            pl.BlockSpec((SEG, 4 * width), lambda d: (d, 0)),
        ],
        out_shape=[
            jax.ShapeDtypeStruct((GROUP * SEG, 2 * width), jnp.bfloat16),
            jax.ShapeDtypeStruct((GROUP * SEG, 4 * width), jnp.bfloat16),
        ],
        cost_estimate=pl.CostEstimate(flops=0, bytes_accessed=24 * GROUP * SEG * width, transcendentals=0),
        name="pack",
    )(*arrays)


def attend_rows(q_ref, row, key_refs):
    joined_q = q_ref[pl.ds(row, ROWS), :]
    plain_q = joined_q[:, DH:]
    nt = (((1,), (1,)), ((), ()))
    scores, tangents = [], []
    for ref, rows in key_refs:
        joined_k = ref[:, 0 : 2 * DH]
        scores.append(lax.dot_general(plain_q, joined_k[:, :DH], nt, preferred_element_type=jnp.float32))
        tangents.append(lax.dot_general(joined_q, joined_k, nt, preferred_element_type=jnp.float32))
    top = functools.reduce(jnp.maximum, [jnp.max(s, axis=-1, keepdims=True) for s in scores])
    expo = [jnp.exp2((s - top) * (SCALE * LOG2E)) for s in scores]
    total = sum(jnp.sum(e, axis=-1, keepdims=True) for e in expo)
    mean = sum(jnp.sum(e * t, axis=-1, keepdims=True) for e, t in zip(expo, tangents)) / total
    both = jnp.zeros((ROWS, 2 * DH), jnp.float32)
    slope = jnp.zeros((ROWS, DH), jnp.float32)
    for (ref, rows), e, t in zip(key_refs, expo, tangents):
        low = e.astype(jnp.bfloat16)
        tan_low = (e * (t - mean)).astype(jnp.bfloat16)
        both = both + jnp.dot(low, ref[:, 2 * DH : 4 * DH], preferred_element_type=jnp.float32)
        slope = slope + jnp.dot(tan_low, ref[:, 2 * DH : 3 * DH], preferred_element_type=jnp.float32)
    inverse = 1.0 / total
    attended = both[:, :DH] * inverse
    attended_tan = (both[:, DH:] + slope * SCALE) * inverse
    log_total = top * SCALE + jnp.log(total)
    log_total_tan = mean * SCALE
    return attended, attended_tan, log_total, log_total_tan


def split3(x):
    high = x.astype(jnp.bfloat16)
    rest = x - high.astype(jnp.float32)
    middle = rest.astype(jnp.bfloat16)
    low = (rest - middle.astype(jnp.float32)).astype(jnp.bfloat16)
    return high, middle, low


def attention(q, kv, before, after, nh):
    def body(q_ref, kv_ref, before_ref, after_ref, out_ref):
        for half, far in enumerate((before_ref, after_ref)):
            for part in range(BLK // ROWS):
                row = half * BLK + part * ROWS
                attended, attended_tan, log_total, log_total_tan = attend_rows(
                    q_ref, row, ((kv_ref, 2 * BLK), (far, BLK))
                )
                lane = lax.broadcasted_iota(jnp.int32, (ROWS, DH), 1)
                stats = jnp.where(lane == 0, log_total, jnp.where(lane == 1, log_total_tan, 0.0))
                stats = jnp.concatenate([part_.astype(jnp.float32) for part_ in split3(stats)], axis=0)
                for s in range(ROWS // SEG):
                    d = row // SEG + s
                    here = slice(s * SEG, (s + 1) * SEG)
                    out_ref[d, 0:SEG, :] = attended[here].astype(jnp.bfloat16)
                    out_ref[d, SEG : 2 * SEG, :] = attended_tan[here].astype(jnp.bfloat16)
                    lines = [stats[p * ROWS + s * SEG : p * ROWS + (s + 1) * SEG].T[0:2] for p in range(3)]
                    lines.append(jnp.zeros((10, SEG), jnp.float32))
                    out_ref[d, 2 * SEG : OUT_ROWS, :] = jnp.concatenate(lines, axis=0).astype(jnp.bfloat16)

    width = 4 * DH
    return pl.pallas_call(
        body,
        grid=(nh,),
        in_specs=[
            pl.BlockSpec((2 * BLK, 2 * DH), lambda h: (0, h)),
            pl.BlockSpec((2 * BLK, width), lambda h: (0, h)),
            pl.BlockSpec((BLK, width), lambda h: (0, h)),
            pl.BlockSpec((BLK, width), lambda h: (0, h)),
        ],
        out_specs=pl.BlockSpec((GROUP, OUT_ROWS, DH), lambda h: (0, 0, h)),
        out_shape=jax.ShapeDtypeStruct((GROUP, OUT_ROWS, nh * DH), jnp.bfloat16),
        compiler_params=pltpu.CompilerParams(vmem_limit_bytes=48 * 1024 * 1024),
        cost_estimate=pl.CostEstimate(
            flops=nh * 2 * 16 * BLK * 3 * BLK * DH, bytes_accessed=nh * 6_000_000, transcendentals=nh * 6 * BLK * BLK
        ),
        name="attention",
    )(q, kv, before, after)


def unpack(chunks, plan):
    def body(*refs):
        parts, (att, att_tan, log_total, log_total_tan) = refs[: len(plan)], refs[len(plan) :]
        lines = []
        for ref, (base, nh) in zip(parts, plan):
            for s in range(GROUP):
                cols = pl.ds((base + s * nh) * DH, nh * DH)
                att[:, cols] = ref[s, 0:SEG, :]
                att_tan[:, cols] = ref[s, SEG : 2 * SEG, :]
                stat = ref[s, 2 * SEG : OUT_ROWS, :].astype(jnp.float32)
                stat = stat[0:2] + (stat[2:4] + stat[4:6])
                lines += [stat[:, j * DH : (j + 1) * DH] for j in range(nh)]
        pad = [jnp.zeros((2 * DH - 2 * len(lines), SEG), jnp.float32)]
        first = jnp.concatenate([line[0:1] for line in lines] + [jnp.zeros((DH - len(lines), SEG), jnp.float32)], axis=0)
        second = jnp.concatenate([line[1:2] for line in lines] + [jnp.zeros((DH - len(lines), SEG), jnp.float32)], axis=0)
        log_total[...] = first.T[:, : len(lines)]
        log_total_tan[...] = second.T[:, : len(lines)]

    heads = GROUP * sum(nh for _, nh in plan)
    return pl.pallas_call(
        body,
        out_shape=[
            jax.ShapeDtypeStruct((SEG, heads * DH), jnp.bfloat16),
            jax.ShapeDtypeStruct((SEG, heads * DH), jnp.bfloat16),
            jax.ShapeDtypeStruct((SEG, heads), jnp.float32),
            jax.ShapeDtypeStruct((SEG, heads), jnp.float32),
        ],
        compiler_params=pltpu.CompilerParams(vmem_limit_bytes=32 * 1024 * 1024),
        cost_estimate=pl.CostEstimate(flops=0, bytes_accessed=4 * SEG * heads * DH * 2, transcendentals=0),
        name="unpack",
    )(*chunks)


def exchange(rows):
    return lax.all_to_all(rows, RING, split_axis=0, concat_axis=0, tiled=True)


def along_line(rows, by, length):
    return lax.ppermute(rows, LINE, [(i, (i + by) % length) for i in range(length)])


def per_device(queries, keys, values, queries_tan, keys_tan, values_tan):
    arrays = (queries, keys, values, queries_tan, keys_tan, values_tan)
    length = lax.axis_size("z") * lax.axis_size("x")
    plan, base = [], 0
    for nh in CHUNKS:
        plan.append((base, nh))
        base += GROUP * nh
    returned = []
    for base, nh in plan:
        q, kv = pack(arrays, base, nh)
        kv = exchange(kv)
        q = exchange(q)
        before = along_line(kv[BLK:], 1, length)
        after = along_line(kv[:BLK], -1, length)
        out = attention(q, kv, before, after, nh)
        returned.append(exchange(out))
    return tuple(unpack(returned, plan))


def solution(mesh):
    inner = Mesh(mesh.devices.reshape(2, 2, 8, 4, 2), AXES)
    placed = P(AXES, None)
    return jax.shard_map(
        per_device,
        mesh=inner,
        in_specs=(placed,) * 6,
        out_specs=(placed,) * 4,
        check_vma=False,
    )
```

time: 768 us -> 218 us (0.28)
  local copies, waits for them, and re-layouts: 253 us -> 7.55 us
  waiting for transfers between devices: 243 us -> 46.7 us
  matrix products: 83.8 us -> 0 us
  blocking collectives: 128 us -> 58.6 us
  Pallas kernels: 0 us -> 51.2 us
  other arithmetic: 36.1 us -> 0 us
  starting transfers between devices: 17 us -> 51.1 us
    ppermute x2 -> x6, waiting for transfers between devices: 214 us -> 9.03 us  [along_line(): lax.ppermute(rows, LINE, [(i, (i + by) % length) for i in range(length)])]
    dynamic_slice x90 -> x0, local copies, waits for them, and re-layouts: 109 us -> none  [attend(): attended, attended_tan, log_total, log_total_tan = lax.map(one_head, pieces)]
    dot_general x40 -> x0, matrix products: 83.8 us -> none  [the longest x10 32.4 us: one_head(): jnp.dot(joined_p, joined_v, preferred_element_type=jnp.float32)]
    all_to_all x1 -> x3, blocking collectives: 128 us -> 58.6 us  [exchange(): return lax.all_to_all(rows, RING, split_axis=0, concat_axis=0, tiled=True)]
    pallas_call x0 -> x7, Pallas kernels: none -> 51.2 us  [the longest x3 31.6 us: attention(): pl.pallas_call(body, grid=(nh,), in_specs=[pl.BlockSpec((2 * BLK, 2 * DH)...]
    slice x10 -> x3, local copies, waits for them, and re-layouts: 41.4 us -> 6.18 us  [per_device(): after = along_line(kv[:BLK], -1, length)]
    dynamic_update_slice x20 -> x0, local copies, waits for them, and re-layouts: 26.7 us -> none  [attend(): attended, attended_tan, log_total, log_total_tan = lax.map(one_head, pieces)]
    all_to_all x2 -> x6, starting transfers between devices: 10 us -> 35.4 us  [exchange(): return lax.all_to_all(rows, RING, split_axis=0, concat_axis=0, tiled=True)]
  transfers between devices with their start and end apart: 4 -> 12, of which waited for: 2 -> 5; matrix products, arithmetic and copies ran while one was open for 2% -> 3% of each run, Pallas kernels for 0% -> 21%
where the time goes in v1:
time: 218 us; the launch traced here: 216 us
  blocking collectives  58.6 us (27%)
  Pallas kernels  51.2 us (23%)
  starting transfers between devices  51.1 us (23%)
  waiting for transfers between devices  46.7 us (21%)
  local copies, waits for them, and re-layouts  7.55 us (3%)
    all_to_all x3, blocking collectives, exchange(): return lax.all_to_all(rows, RING, split_axis=0, concat_axis=0, tiled=True)  58.6 us
    all_to_all x6, waiting for transfers between devices, exchange(): return lax.all_to_all(rows, RING, split_axis=0, concat_axis=0, tiled=True)  37.7 us
    all_to_all x6, starting transfers between devices, exchange(): return lax.all_to_all(rows, RING, split_axis=0, concat_axis=0, tiled=True)  35.4 us
    pallas_call x3, Pallas kernels, attention(): pl.pallas_call(body, grid=(nh,), in_specs=[pl.BlockSpec((2 * BLK, 2 * DH)...  31.6 us
    pallas_call x3, Pallas kernels, pack(): pl.pallas_call(body, grid=(GROUP,), in_specs=[spec] * 6, out_specs=[pl.Bl...  17.9 us
    ppermute x6, starting transfers between devices, along_line(): lax.ppermute(rows, LINE, [(i, (i + by) % length) for i in range(length)])  15.6 us
    ppermute x6, waiting for transfers between devices, along_line(): lax.ppermute(rows, LINE, [(i, (i + by) % length) for i in range(length)])  9.03 us
    slice x3, local copies, waits for them, and re-layouts, per_device(): after = along_line(kv[:BLK], -1, length)  6.18 us
  transfers between devices with their start and end apart: 12, of which 5 were waited for; matrix products, arithmetic and copies ran while one was open for 3% of the time, Pallas kernels for 21%

profile of v1, /device:TPU:1, one launch (start us, length us, event | category | flops | bytes accessed | tf_op | source)
XLA Modules:
  0.0 215.8 jit_solution(15033754183030231070)
XLA Ops:
  0.6 5.2 %pack.5 = (bf16[1024,256]{1,0:T(8,128)(2,1)}, bf16[1024,512]{1,0:T(8,128)(2,1)}) custom-call(bf16[128,5120]{1,0:T(8,128)(2,1)} %q.5, bf16[128,5120]{1,0:T(8,128)(2,1)} %k.5, bf16[128,5120]{1,0:T(8,128)(2,1)} %v.5, bf16[128,5120]{1,0:T(8,128)(2,1)} %dq.5, bf16[128,5120]{1,0:T(8,128)(2,1)} %dk.5, bf16[128,5120]{1,0:T(8,128)(2,1)} %dv.5), custom_call_target="tpu_custom_call" | custom-call | bytes 3145728 | tf_op jit(solution)/shard_map/pack/pallas_call | solution.py:39
  5.8 6.6 %all-to-all-start.6 = ((bf16[8,128,256]{2,1,0:T(8,128)(2,1)}), bf16[8,128,256]{2,1,0:T(8,128)(2,1)S(1)}, u32[]{:S(2)}, u32[]{:S(2)}) async-start(bf16[8,128,256]{2,1,0:T(8,128)(2,1)} %bitcast.26), calls=%async_computation.6 | async-start | bytes 1048576 | tf_op jit(solution)/shard_map/all_to_all | solution.py:166
  12.4 6.3 %pack.3 = (bf16[1024,512]{1,0:T(8,128)(2,1)}, bf16[1024,1024]{1,0:T(8,128)(2,1)}) custom-call(bf16[128,5120]{1,0:T(8,128)(2,1)} %q.5, bf16[128,5120]{1,0:T(8,128)(2,1)} %k.5, bf16[128,5120]{1,0:T(8,128)(2,1)} %v.5, bf16[128,5120]{1,0:T(8,128)(2,1)} %dq.5, bf16[128,5120]{1,0:T(8,128)(2,1)} %dk.5, bf16[128,5120]{1,0:T(8,128)(2,1)} %dv.5), custom_call_target="tpu_custom_call" | custom-call | bytes 6291456 | tf_op jit(solution)/shard_map/pack/pallas_call | solution.py:39
  18.8 2.4 %all-to-all-done.6 = bf16[8,128,256]{2,1,0:T(8,128)(2,1)S(1)} async-done(((bf16[8,128,256]{2,1,0:T(8,128)(2,1)}), bf16[8,128,256]{2,1,0:T(8,128)(2,1)S(1)}, u32[]{:S(2)}, u32[]{:S(2)}) %all-to-all-start.6) | async-done | bytes 524320 | tf_op jit(solution)/shard_map/all_to_all | solution.py:166
  21.2 19.7 %all_to_all.81 = bf16[8,128,512]{2,1,0:T(8,128)(2,1)S(1)} all-to-all(bf16[8,128,512]{2,1,0:T(8,128)(2,1)} %bitcast.25), channel_id=1, replica_groups=mesh['y_hi'=2,'core'=2,'z'=8,'x'=4,'y_lo'=2] {'y_lo','y_hi','core'}, dimensions={0} | all-to-all | bytes 2097152 | tf_op jit(solution)/shard_map/all_to_all | solution.py:166
  40.9 18.4 %all_to_all.82 = bf16[8,128,512]{2,1,0:T(8,128)(2,1)S(1)} all-to-all(bf16[8,128,512]{2,1,0:T(8,128)(2,1)S(1)} %bitcast.24), channel_id=1, replica_groups=mesh['y_hi'=2,'core'=2,'z'=8,'x'=4,'y_lo'=2] {'y_lo','y_hi','core'}, dimensions={0} | all-to-all | bytes 2097152 | tf_op jit(solution)/shard_map/all_to_all | solution.py:166
  59.3 5.1 %all-to-all-start.1 = ((bf16[8,128,1024]{2,1,0:T(8,128)(2,1)}), bf16[8,128,1024]{2,1,0:T(8,128)(2,1)}, u32[]{:S(2)}, u32[]{:S(2)}) async-start(bf16[8,128,1024]{2,1,0:T(8,128)(2,1)} %bitcast.22), calls=%async_computation.1 | async-start | bytes 4194304 | tf_op jit(solution)/shard_map/all_to_all | solution.py:166
  64.4 6.3 %pack.4 = (bf16[1024,512]{1,0:T(8,128)(2,1)}, bf16[1024,1024]{1,0:T(8,128)(2,1)}) custom-call(bf16[128,5120]{1,0:T(8,128)(2,1)} %q.5, bf16[128,5120]{1,0:T(8,128)(2,1)} %k.5, bf16[128,5120]{1,0:T(8,128)(2,1)} %v.5, bf16[128,5120]{1,0:T(8,128)(2,1)} %dq.5, bf16[128,5120]{1,0:T(8,128)(2,1)} %dk.5, bf16[128,5120]{1,0:T(8,128)(2,1)} %dv.5), custom_call_target="tpu_custom_call" | custom-call | bytes 6291456 | tf_op jit(solution)/shard_map/pack/pallas_call | solution.py:39
  70.8 18.6 %all-to-all-done.1 = bf16[8,128,1024]{2,1,0:T(8,128)(2,1)} async-done(((bf16[8,128,1024]{2,1,0:T(8,128)(2,1)}), bf16[8,128,1024]{2,1,0:T(8,128)(2,1)}, u32[]{:S(2)}, u32[]{:S(2)}) %all-to-all-start.1) | async-done | bytes 2097184 | tf_op jit(solution)/shard_map/all_to_all | solution.py:166
  89.4 6.3 %all-to-all-start.4 = ((bf16[8,128,1024]{2,1,0:T(8,128)(2,1)}), bf16[8,128,1024]{2,1,0:T(8,128)(2,1)}, u32[]{:S(2)}, u32[]{:S(2)}) async-start(bf16[8,128,1024]{2,1,0:T(8,128)(2,1)} %bitcast.21), calls=%async_computation.4 | async-start | bytes 4194304 | tf_op jit(solution)/shard_map/all_to_all | solution.py:166
  95.7 3.0 %fusion.1 = (bf16[4,128,1024]{2,1,0:T(8,128)(2,1)}, bf16[4,128,1024]{2,1,0:T(8,128)(2,1)}) fusion(bf16[8,128,1024]{2,1,0:T(8,128)(2,1)} %all-to-all-done.1), kind=kLoop, calls=%fused_computation.1 | loop fusion | bytes 4194304 | tf_op jit(solution)/shard_map/slice | solution.py:186
  98.7 0.5 collective-permute-start
  99.2 6.6 %collective-permute-start.1 = (bf16[512,1024]{1,0:T(8,128)(2,1)}, bf16[512,1024]{1,0:T(8,128)(2,1)}, u32[]{:S(2)}, u32[]{:S(2)}) collective-permute-start(bf16[512,1024]{1,0:T(8,128)(2,1)} %bitcast.5), channel_id=1, source_target_pairs={{0,62},{2,0},{4,2},{6,4},{8,6},{10,8},{12,10},{14,12},{16,14},{18,... | collective-permute-start | bytes 3145736 | tf_op jit(solution)/shard_map/ppermute | solution.py:170
  105.8 14.8 %all-to-all-done.4 = bf16[8,128,1024]{2,1,0:T(8,128)(2,1)} async-done(((bf16[8,128,1024]{2,1,0:T(8,128)(2,1)}), bf16[8,128,1024]{2,1,0:T(8,128)(2,1)}, u32[]{:S(2)}, u32[]{:S(2)}) %all-to-all-start.4) | async-done | bytes 2097184 | tf_op jit(solution)/shard_map/all_to_all | solution.py:166
  120.6 6.2 %all-to-all-start.3 = ((bf16[8,128,512]{2,1,0:T(8,128)(2,1)}), bf16[8,128,512]{2,1,0:T(8,128)(2,1)}, u32[]{:S(2)}, u32[]{:S(2)}) async-start(bf16[8,128,512]{2,1,0:T(8,128)(2,1)} %bitcast.23), calls=%async_computation.3 | async-start | bytes 2097152 | tf_op jit(solution)/shard_map/all_to_all | solution.py:166
  126.9 0.1 fusion.2
  127.0 0.6 collective-permute-start.4
  127.6 6.6 %collective-permute-start.5 = (bf16[512,512]{1,0:T(8,128)(2,1)S(1)}, bf16[512,512]{1,0:T(8,128)(2,1)S(1)}, u32[]{:S(2)}, u32[]{:S(2)}) collective-permute-start(bf16[512,512]{1,0:T(8,128)(2,1)S(1)} %bitcast.27), channel_id=1, source_target_pairs={{0,62},{2,0},{4,2},{6,4},{8,6},{10,8},{12,10},{14,12},{16,14},{18,... | collective-permute-start | bytes 1572872 | tf_op jit(solution)/shard_map/ppermute | solution.py:170
  134.2 3.1 %fusion = (bf16[4,128,1024]{2,1,0:T(8,128)(2,1)}, bf16[4,128,1024]{2,1,0:T(8,128)(2,1)}) fusion(bf16[8,128,1024]{2,1,0:T(8,128)(2,1)} %all-to-all-done.4), kind=kLoop, calls=%fused_computation | loop fusion | bytes 4194304 | tf_op jit(solution)/shard_map/slice | solution.py:186
  137.3 0.0 collective-permute-start.2
  137.3 9.0 %collective-permute-done.4.before_ref = bf16[512,512]{1,0:T(8,128)(2,1)S(1)} collective-permute-done((bf16[512,512]{1,0:T(8,128)(2,1)S(1)}, bf16[512,512]{1,0:T(8,128)(2,1)S(1)}, u32[]{:S(2)}, u32[]{:S(2)}) %collective-permute-start.4) | collective-permute-done | bytes 524320 | tf_op jit(solution)/shard_map/ppermute | solution.py:170
  146.3 1.3 collective-permute-start.3
  147.6 6.2 %attention.5 = bf16[8,272,128]{2,1,0:T(8,128)(2,1)} custom-call(bf16[1024,256]{1,0:T(8,128)(2,1)S(1)} %bitcast.20, bf16[1024,512]{1,0:T(8,128)(2,1)S(1)} %bitcast.18, bf16[512,512]{1,0:T(8,128)(2,1)S(1)} %collective-permute-done.4.before_ref, bf16[512,512]{1,0:T(8,128)(2,1)S(1)} %collective-permute-done.5.after_ref), custom_call_target="tpu_custom_call" | custom-call | flops 3221225472 | bytes 6000000 | tf_op jit(solution)/shard_map/attention/pallas_call | solution.py:113
  153.8 6.4 %all-to-all-start.8 = ((bf16[8,272,128]{2,1,0:T(8,128)(2,1)}), bf16[8,272,128]{2,1,0:T(8,128)(2,1)S(1)}, u32[]{:S(2)}, u32[]{:S(2)}) async-start(bf16[8,272,128]{2,1,0:T(8,128)(2,1)} %attention.5), calls=%async_computation.8 | async-start | bytes 1114112 | tf_op jit(solution)/shard_map/all_to_all | solution.py:166
  160.2 13.0 %attention.3 = bf16[8,272,256]{2,1,0:T(8,128)(2,1)} custom-call(bf16[1024,512]{1,0:T(8,128)(2,1)S(1)} %bitcast.19, bf16[1024,1024]{1,0:T(8,128)(2,1)} %bitcast.3.kv_ref, bf16[512,1024]{1,0:T(8,128)(2,1)} %collective-permute-done.before_ref, bf16[512,1024]{1,0:T(8,128)(2,1)} %collective-permute-done.1.after_ref), custom_call_target="tpu_custom_call" | custom-call | flops 6442450944 | bytes 12000000 | tf_op jit(solution)/shard_map/attention/pallas_call | solution.py:113
  173.1 4.8 %all-to-all-start.2 = ((bf16[8,272,256]{2,1,0:T(8,128)(2,1)}), bf16[8,272,256]{2,1,0:T(8,128)(2,1)S(1)}, u32[]{:S(2)}, u32[]{:S(2)}) async-start(bf16[8,272,256]{2,1,0:T(8,128)(2,1)} %attention.3), calls=%async_computation.2 | async-start | bytes 2228224 | tf_op jit(solution)/shard_map/all_to_all | solution.py:166
  178.0 12.5 %attention.4 = bf16[8,272,256]{2,1,0:T(8,128)(2,1)S(1)} custom-call(bf16[1024,512]{1,0:T(8,128)(2,1)} %bitcast.7.q_ref, bf16[1024,1024]{1,0:T(8,128)(2,1)} %bitcast.9.kv_ref, bf16[512,1024]{1,0:T(8,128)(2,1)} %collective-permute-done.2.before_ref, bf16[512,1024]{1,0:T(8,128)(2,1)} %collective-permute-done.3.after_ref), custom_call_target="tpu_custom_call" | custom-call | flops 6442450944 | bytes 12000000 | tf_op jit(solution)/shard_map/attention/pallas_call | solution.py:113
  190.5 1.8 all-to-all-done.2.refs_0_
  192.3 20.5 %all_to_all.83.refs_1_ = bf16[8,272,256]{2,1,0:T(8,128)(2,1)S(1)} all-to-all(bf16[8,272,256]{2,1,0:T(8,128)(2,1)S(1)} %attention.4), channel_id=1, replica_groups=mesh['y_hi'=2,'core'=2,'z'=8,'x'=4,'y_lo'=2] {'y_lo','y_hi','core'}, dimensions={0} | all-to-all | bytes 2228224 | tf_op jit(solution)/shard_map/all_to_all | solution.py:166
  212.8 1.7 unpack.1
  214.5 0.7 copy.10
  215.1 0.7 copy.11
  (9 shorter events, 0.0 us)
Async XLA Ops:
  5.8 15.4 %all-to-all-start.6 = ((bf16[8,128,256]{2,1,0:T(8,128)(2,1)}), bf16[8,128,256]{2,1,0:T(8,128)(2,1)S(1)}, u32[]{:S(2)}, u32[]{:S(2)}) async-start(bf16[8,128,256]{2,1,0:T(8,128)(2,1)} %bitcast.26), calls=%async_computation.6 | async-start | bytes 1048576 | tf_op jit(solution)/shard_map/all_to_all | solution.py:166
  21.2 19.7 %copy-start = (bf16[1024,512]{1,0:T(8,128)(2,1)S(1)}, bf16[1024,512]{1,0:T(8,128)(2,1)}, u32[]{:S(2)}) copy-start(bf16[1024,512]{1,0:T(8,128)(2,1)} %get-tuple-element.15) | copy-start | bytes 3145732
  59.3 30.0 %all-to-all-start.1 = ((bf16[8,128,1024]{2,1,0:T(8,128)(2,1)}), bf16[8,128,1024]{2,1,0:T(8,128)(2,1)}, u32[]{:S(2)}, u32[]{:S(2)}) async-start(bf16[8,128,1024]{2,1,0:T(8,128)(2,1)} %bitcast.22), calls=%async_computation.1 | async-start | bytes 4194304 | tf_op jit(solution)/shard_map/all_to_all | solution.py:166
  89.4 31.3 %all-to-all-start.4 = ((bf16[8,128,1024]{2,1,0:T(8,128)(2,1)}), bf16[8,128,1024]{2,1,0:T(8,128)(2,1)}, u32[]{:S(2)}, u32[]{:S(2)}) async-start(bf16[8,128,1024]{2,1,0:T(8,128)(2,1)} %bitcast.21), calls=%async_computation.4 | async-start | bytes 4194304 | tf_op jit(solution)/shard_map/all_to_all | solution.py:166
  98.7 61.4 %collective-permute-start = (bf16[512,1024]{1,0:T(8,128)(2,1)}, bf16[512,1024]{1,0:T(8,128)(2,1)}, u32[]{:S(2)}, u32[]{:S(2)}) collective-permute-start(bf16[512,1024]{1,0:T(8,128)(2,1)} %bitcast.4), channel_id=1, source_target_pairs={{0,2},{2,4},{4,6},{6,8},{8,10},{10,12},{12,14},{14,16},{16,18},{18... | collective-permute-start | bytes 3145736 | tf_op jit(solution)/shard_map/ppermute | solution.py:170
  99.2 60.9 %collective-permute-start.1 = (bf16[512,1024]{1,0:T(8,128)(2,1)}, bf16[512,1024]{1,0:T(8,128)(2,1)}, u32[]{:S(2)}, u32[]{:S(2)}) collective-permute-start(bf16[512,1024]{1,0:T(8,128)(2,1)} %bitcast.5), channel_id=1, source_target_pairs={{0,62},{2,0},{4,2},{6,4},{8,6},{10,8},{12,10},{14,12},{16,14},{18,... | collective-permute-start | bytes 3145736 | tf_op jit(solution)/shard_map/ppermute | solution.py:170
  120.6 33.1 %all-to-all-start.3 = ((bf16[8,128,512]{2,1,0:T(8,128)(2,1)}), bf16[8,128,512]{2,1,0:T(8,128)(2,1)}, u32[]{:S(2)}, u32[]{:S(2)}) async-start(bf16[8,128,512]{2,1,0:T(8,128)(2,1)} %bitcast.23), calls=%async_computation.3 | async-start | bytes 2097152 | tf_op jit(solution)/shard_map/all_to_all | solution.py:166
  127.0 19.3 %collective-permute-start.4 = (bf16[512,512]{1,0:T(8,128)(2,1)S(1)}, bf16[512,512]{1,0:T(8,128)(2,1)S(1)}, u32[]{:S(2)}, u32[]{:S(2)}) collective-permute-start(bf16[512,512]{1,0:T(8,128)(2,1)S(1)} %bitcast.28), channel_id=1, source_target_pairs={{0,2},{2,4},{4,6},{6,8},{8,10},{10,12},{12,14},{14,16},{16,18},{18... | collective-permute-start | bytes 1572872 | tf_op jit(solution)/shard_map/ppermute | solution.py:170
  127.6 20.1 %collective-permute-start.5 = (bf16[512,512]{1,0:T(8,128)(2,1)S(1)}, bf16[512,512]{1,0:T(8,128)(2,1)S(1)}, u32[]{:S(2)}, u32[]{:S(2)}) collective-permute-start(bf16[512,512]{1,0:T(8,128)(2,1)S(1)} %bitcast.27), channel_id=1, source_target_pairs={{0,62},{2,0},{4,2},{6,4},{8,6},{10,8},{12,10},{14,12},{16,14},{18,... | collective-permute-start | bytes 1572872 | tf_op jit(solution)/shard_map/ppermute | solution.py:170
  137.3 40.7 %collective-permute-start.2 = (bf16[512,1024]{1,0:T(8,128)(2,1)}, bf16[512,1024]{1,0:T(8,128)(2,1)}, u32[]{:S(2)}, u32[]{:S(2)}) collective-permute-start(bf16[512,1024]{1,0:T(8,128)(2,1)} %bitcast.10), channel_id=1, source_target_pairs={{0,2},{2,4},{4,6},{6,8},{8,10},{10,12},{12,14},{14,16},{16,18},{18... | collective-permute-start | bytes 3145736 | tf_op jit(solution)/shard_map/ppermute | solution.py:170
  146.3 31.7 %collective-permute-start.3 = (bf16[512,1024]{1,0:T(8,128)(2,1)}, bf16[512,1024]{1,0:T(8,128)(2,1)}, u32[]{:S(2)}, u32[]{:S(2)}) collective-permute-start(bf16[512,1024]{1,0:T(8,128)(2,1)} %bitcast.11), channel_id=1, source_target_pairs={{0,62},{2,0},{4,2},{6,4},{8,6},{10,8},{12,10},{14,12},{16,14},{18,... | collective-permute-start | bytes 3145736 | tf_op jit(solution)/shard_map/ppermute | solution.py:170
  153.8 19.4 %all-to-all-start.8 = ((bf16[8,272,128]{2,1,0:T(8,128)(2,1)}), bf16[8,272,128]{2,1,0:T(8,128)(2,1)S(1)}, u32[]{:S(2)}, u32[]{:S(2)}) async-start(bf16[8,272,128]{2,1,0:T(8,128)(2,1)} %attention.5), calls=%async_computation.8 | async-start | bytes 1114112 | tf_op jit(solution)/shard_map/all_to_all | solution.py:166
  173.1 19.1 %all-to-all-start.2 = ((bf16[8,272,256]{2,1,0:T(8,128)(2,1)}), bf16[8,272,256]{2,1,0:T(8,128)(2,1)S(1)}, u32[]{:S(2)}, u32[]{:S(2)}) async-start(bf16[8,272,256]{2,1,0:T(8,128)(2,1)} %attention.3), calls=%async_computation.2 | async-start | bytes 2228224 | tf_op jit(solution)/shard_map/all_to_all | solution.py:166

commit v2 on v1

v2 whole, which is shorter than its diff:
```python
import functools

import jax
import jax.numpy as jnp
from jax import lax
from jax.experimental import pallas as pl
from jax.experimental.pallas import tpu as pltpu
from jax.sharding import Mesh, PartitionSpec as P

DH = 128
SEG = 128
BLK = 512
ROWS = 256
SLOTS = 4
OUT_ROWS = 2 * SEG + 16
SCALE = 1.0 / DH**0.5
LOG2E = 1.4426950408889634
AXES = ("y_hi", "core", "z", "x", "y_lo")
RING = ("y_hi", "core", "y_lo")
LINE = ("core", "z", "x")
STEPS = ((1, 2, 3, 0), (2, 3, 0, 1))
CHUNKS = (4, 4, 2)
WINDOW = 4
GATHER = False
ORDER = (
    ("pack", 0),
    ("pack", 0),
    ("pack", 0),
    ("pack", 0),
    ("pack", 0),
    ("pack", 0),
    ("pack", 0),
    ("pack", 0),
    ("join", 0),
    ("pack", 0),
    ("pack", 0),
    ("pack", 0),
    ("pack", 0),
    ("join", 1),
    ("attend", 0),
    ("join", 2),
    ("attend", 1),
    ("attend", 2),
)
ANY = pl.BlockSpec(memory_space=pl.ANY)
HBM = pl.BlockSpec(memory_space=pltpu.HBM)
VMEM = pl.BlockSpec(memory_space=pltpu.VMEM)
MIB = 1024 * 1024


def slot_chip(k):
    y = 2 * lax.axis_index("y_hi") + lax.axis_index("y_lo")
    return (y + jnp.where(lax.axis_index("core") == 0, STEPS[0][k], STEPS[1][k])) % 4


def slot_pairs(k):
    pairs = []
    for y_hi in range(2):
        for core in range(2):
            for y_lo in range(2):
                y = (2 * y_hi + y_lo + STEPS[core][k]) % 4
                pairs.append((4 * y_hi + 2 * core + y_lo, 4 * (y // 2) + 2 * y_lo + y % 2))
    return pairs


def outer_pairs(length):
    return [(length + s, (s + 1) % length) for s in range(length)] + [
        (s, length + (s - 1) % length) for s in range(length)
    ]


def pack(arrays, base, nh, k, after):
    width = nh * DH

    def body(*refs):
        ins, (out, held, into, out_of) = refs[:6], refs[6 + len(after) :]
        first = pl.multiple_of((base + slot_chip(k) * nh) * DH, DH)
        loads = []
        for i, ref in enumerate(ins):
            load = pltpu.make_async_copy(
                ref.at[:, pl.ds(first, width)], held.at[:, pl.ds(i * width, width)], into.at[i]
            )
            load.start()
            loads.append(load)
        for load in loads:
            load.wait()
        store = pltpu.make_async_copy(held, out, out_of)
        store.start()
        store.wait()

    return pl.pallas_call(
        body,
        in_specs=[HBM] * 6 + [ANY] * len(after),
        out_specs=ANY,
        out_shape=jax.ShapeDtypeStruct((SEG, 6 * width), jnp.bfloat16),
        scratch_shapes=[
            pltpu.VMEM((SEG, 6 * width), jnp.bfloat16),
            pltpu.SemaphoreType.DMA((6,)),
            pltpu.SemaphoreType.DMA,
        ],
        compiler_params=pltpu.CompilerParams(vmem_limit_bytes=(16 if base else 60) * MIB),
        cost_estimate=pl.CostEstimate(flops=0, bytes_accessed=24 * SEG * width, transcendentals=0),
        name="pack",
    )(*arrays, *after)


def join(messages, nh, after):
    width = 4 * nh * DH

    def body(*refs):
        out = refs[-1]
        for k in range(SLOTS):
            out[k * SEG : (k + 1) * SEG, :] = refs[k][:, 2 * nh * DH :]

    return pl.pallas_call(
        body,
        in_specs=[VMEM] * SLOTS + [ANY] * len(after),
        out_specs=VMEM,
        out_shape=jax.ShapeDtypeStruct((BLK, width), jnp.bfloat16),
        compiler_params=pltpu.CompilerParams(vmem_limit_bytes=16 * MIB),
        cost_estimate=pl.CostEstimate(flops=0, bytes_accessed=4 * BLK * width, transcendentals=0),
        name="join",
    )(*messages, *after)


def attend_rows(plain_q, joined_q, key_refs):
    nt = (((1,), (1,)), ((), ()))
    scores, tangents = [], []
    for k, dk, v, dv in key_refs:
        plain_k = k[...]
        joined_k = jnp.concatenate([plain_k, dk[...]], axis=1)
        scores.append(lax.dot_general(plain_q, plain_k, nt, preferred_element_type=jnp.float32))
        tangents.append(lax.dot_general(joined_q, joined_k, nt, preferred_element_type=jnp.float32))
    top = functools.reduce(jnp.maximum, [jnp.max(s, axis=-1, keepdims=True) for s in scores])
    expo = [jnp.exp2((s - top) * (SCALE * LOG2E)) for s in scores]
    total = sum(jnp.sum(e, axis=-1, keepdims=True) for e in expo)
    mean = sum(jnp.sum(e * t, axis=-1, keepdims=True) for e, t in zip(expo, tangents)) / total
    both = jnp.zeros((ROWS, 2 * DH), jnp.float32)
    slope = jnp.zeros((ROWS, DH), jnp.float32)
    for (k, dk, v, dv), e, t in zip(key_refs, expo, tangents):
        low = e.astype(jnp.bfloat16)
        tan_low = (e * (t - mean)).astype(jnp.bfloat16)
        joined_v = jnp.concatenate([v[...], dv[...]], axis=1)
        both = both + jnp.dot(low, joined_v, preferred_element_type=jnp.float32)
        slope = slope + jnp.dot(tan_low, v[...], preferred_element_type=jnp.float32)
    inverse = 1.0 / total
    attended = both[:, :DH] * inverse
    attended_tan = (both[:, DH:] + slope * SCALE) * inverse
    log_total = top * SCALE + jnp.log(total)
    log_total_tan = mean * SCALE
    return attended, attended_tan, log_total, log_total_tan


def split3(x):
    high = x.astype(jnp.bfloat16)
    rest = x - high.astype(jnp.float32)
    middle = rest.astype(jnp.bfloat16)
    low = (rest - middle.astype(jnp.float32)).astype(jnp.bfloat16)
    return high, middle, low


def attention(messages, keysets, nh, after):
    def body(*refs):
        tan_refs, q_refs, refs = refs[:SLOTS], refs[SLOTS : 2 * SLOTS], refs[2 * SLOTS :]
        key_refs = [refs[4 * i : 4 * i + 4] for i in range(len(keysets))]
        outs = refs[4 * len(keysets) + len(after) :]
        per = ROWS // SEG
        for part in range(BLK // ROWS):
            here = range(part * per, part * per + per)
            plain_q = jnp.concatenate([q_refs[k][...] for k in here], axis=0)
            tan_q = jnp.concatenate([tan_refs[k][...] for k in here], axis=0)
            joined_q = jnp.concatenate([tan_q, plain_q], axis=1)
            attended, attended_tan, log_total, log_total_tan = attend_rows(plain_q, joined_q, key_refs)
            lane = lax.broadcasted_iota(jnp.int32, (ROWS, DH), 1)
            stats = jnp.where(lane == 0, log_total, jnp.where(lane == 1, log_total_tan, 0.0))
            pieces = [piece.astype(jnp.float32) for piece in split3(stats)]
            for s, k in enumerate(here):
                rows = slice(s * SEG, (s + 1) * SEG)
                outs[k][0:SEG, :] = attended[rows].astype(jnp.bfloat16)
                outs[k][SEG : 2 * SEG, :] = attended_tan[rows].astype(jnp.bfloat16)
                lines = [piece[rows].T[0:2] for piece in pieces]
                lines.append(jnp.zeros((10, SEG), jnp.float32))
                outs[k][2 * SEG : OUT_ROWS, :] = jnp.concatenate(lines, axis=0).astype(jnp.bfloat16)

    def columns(rows, i):
        return pl.BlockSpec((rows, DH), lambda h: (0, i * nh + h))

    return pl.pallas_call(
        body,
        grid=(nh,),
        in_specs=[columns(SEG, 0)] * SLOTS
        + [columns(SEG, 1)] * SLOTS
        + [columns(keyset.shape[0], i) for keyset in keysets for i in range(4)]
        + [ANY] * len(after),
        out_specs=[columns(OUT_ROWS, 0)] * SLOTS,
        out_shape=[jax.ShapeDtypeStruct((OUT_ROWS, nh * DH), jnp.bfloat16)] * SLOTS,
        compiler_params=pltpu.CompilerParams(vmem_limit_bytes=20 * MIB),
        cost_estimate=pl.CostEstimate(
            flops=nh * 2 * 16 * BLK * 3 * BLK * DH // 2,
            bytes_accessed=nh * 2_500_000,
            transcendentals=nh * 3 * BLK * BLK,
        ),
        name="attention",
    )(*messages, *messages, *[keyset for keyset in keysets for _ in range(4)], *after)


def unpack(chunks, plan):
    def body(*refs):
        chips = [slot_chip(k) for k in range(SLOTS)]
        parts, (att, att_tan, log_total, log_total_tan) = refs[: SLOTS * len(plan)], refs[SLOTS * len(plan) : -1]
        lines = refs[-1]
        for c, (base, nh) in enumerate(plan):
            for k in range(SLOTS):
                ref = parts[c * SLOTS + k]
                head = base + chips[k] * nh
                cols = pl.ds(pl.multiple_of(head * DH, DH), nh * DH)
                att[:, cols] = ref[0:SEG, :]
                att_tan[:, cols] = ref[SEG : 2 * SEG, :]
                stat = ref[2 * SEG : OUT_ROWS, :].astype(jnp.float32)
                stat = stat[0:2] + (stat[2:4] + stat[4:6])
                for j in range(nh):
                    lines[0, pl.ds(head + j, 1), :] = stat[0:1, j * DH : (j + 1) * DH]
                    lines[1, pl.ds(head + j, 1), :] = stat[1:2, j * DH : (j + 1) * DH]
        log_total[...] = lines[0]
        log_total_tan[...] = lines[1]

    heads = SLOTS * sum(nh for _, nh in plan)
    whole = pl.BlockSpec(memory_space=pltpu.VMEM)
    return pl.pallas_call(
        body,
        in_specs=[whole] * (SLOTS * len(plan)),
        out_specs=[whole] * 4,
        out_shape=[
            jax.ShapeDtypeStruct((SEG, heads * DH), jnp.bfloat16),
            jax.ShapeDtypeStruct((SEG, heads * DH), jnp.bfloat16),
            jax.ShapeDtypeStruct((heads, SEG), jnp.float32),
            jax.ShapeDtypeStruct((heads, SEG), jnp.float32),
        ],
        scratch_shapes=[pltpu.VMEM((2, heads, SEG), jnp.float32)],
        compiler_params=pltpu.CompilerParams(vmem_limit_bytes=16 * MIB),
        cost_estimate=pl.CostEstimate(flops=0, bytes_accessed=4 * SEG * heads * DH * 2, transcendentals=0),
        name="unpack",
    )(*chunks)


def per_device(queries, keys, values, queries_tan, keys_tan, values_tan):
    arrays = (queries_tan, queries, keys, keys_tan, values, values_tan)
    length = lax.axis_size("z") * lax.axis_size("x")
    there = [slot_pairs(k) for k in range(SLOTS)]
    back = [[(b, a) for a, b in pairs] for pairs in there]
    plan, base = [], 0
    for nh in CHUNKS:
        plan.append((base, nh))
        base += SLOTS * nh
    n = len(plan)
    arrived, joined, others, returned = [], [None] * n, [None] * n, [None] * n
    last = []
    for kind, c in ORDER:
        if kind == "pack":
            m, k = len(arrived), len(arrived) % SLOTS
            base, nh = plan[m // SLOTS]
            after = last + ([arrived[m - WINDOW]] if m >= WINDOW else [])
            sent = pack(arrays, base, nh, k, after)
            arrived.append(lax.ppermute(sent, RING, there[k]))
            last = [sent]
            continue
        base, nh = plan[c]
        messages = arrived[SLOTS * c : SLOTS * c + SLOTS]
        if kind == "join":
            joined[c] = join(messages, nh, last)
            outer = lax.ppermute(joined[c], LINE, outer_pairs(length))
            if GATHER:
                others[c] = (lax.all_gather(joined[c], "core", axis=0, tiled=True), outer)
            else:
                others[c] = (joined[c], lax.ppermute(joined[c], "core", [(0, 1), (1, 0)]), outer)
            last = [joined[c]]
        else:
            outs = attention(messages, others[c], nh, last)
            returned[c] = [lax.ppermute(outs[k], RING, back[k]) for k in range(SLOTS)]
            last = [outs[0]]
    att, att_tan, log_total, log_total_tan = unpack([part for parts in returned for part in parts], plan)
    return att, att_tan, log_total.T, log_total_tan.T


def solution(mesh):
    inner = Mesh(mesh.devices.reshape(2, 2, 8, 4, 2), AXES)
    placed = P(AXES, None)
    return jax.shard_map(
        per_device,
        mesh=inner,
        in_specs=(placed,) * 6,
        out_specs=(placed,) * 4,
        check_vma=False,
    )
```

time: 218 us -> 176 us (0.81)
  blocking collectives: 58.6 us -> 0 us
  starting transfers between devices: 51.1 us -> 72.6 us
  Pallas kernels: 51.2 us -> 48.1 us
  local copies, waits for them, and re-layouts: 7.55 us -> 5.11 us
    all_to_all x3 -> x0, blocking collectives: 58.6 us -> none  [exchange(): return lax.all_to_all(rows, RING, split_axis=0, concat_axis=0, tiled=True)]
    ppermute x6 -> x30, starting transfers between devices: 15.6 us -> 72.6 us  [the longest x12 42.8 us: per_device(): arrived.append(lax.ppermute(sent, RING, there[k]))]
    ppermute x6 -> x30, waiting for transfers between devices: 9.03 us -> 48 us  [the longest x12 42.4 us: per_device(): arrived.append(lax.ppermute(sent, RING, there[k]))]
    all_to_all x6 -> x0, waiting for transfers between devices: 37.7 us -> none  [exchange(): return lax.all_to_all(rows, RING, split_axis=0, concat_axis=0, tiled=True)]
    all_to_all x6 -> x0, starting transfers between devices: 35.4 us -> none  [exchange(): return lax.all_to_all(rows, RING, split_axis=0, concat_axis=0, tiled=True)]
    slice x3 -> x0, local copies, waits for them, and re-layouts: 6.18 us -> none  [per_device(): after = along_line(kv[:BLK], -1, length)]
    unnamed x2 -> x20, local copies, waits for them, and re-layouts: 0.01 us -> 5.11 us
    pallas_call x7 -> x19, Pallas kernels: 51.2 us -> 48.1 us  [the longest x3 33.5 us: attention(): pl.pallas_call(body, grid=(nh,), in_specs=[columns(SEG, 0)] * SLOTS + [co...]
  transfers between devices with their start and end apart: 12 -> 30, of which waited for: 5 -> 11; matrix products, arithmetic and copies ran while one was open for 3% -> 0% of each run, Pallas kernels for 21% -> 25%
where the time goes in v2:
time: 176 us; the launch traced here: 175 us
  starting transfers between devices  72.6 us (41%)
  Pallas kernels  48.1 us (27%)
  waiting for transfers between devices  48 us (27%)
  local copies, waits for them, and re-layouts  5.11 us (3%)
    ppermute x12, starting transfers between devices, per_device(): arrived.append(lax.ppermute(sent, RING, there[k]))  42.8 us
    ppermute x12, waiting for transfers between devices, per_device(): arrived.append(lax.ppermute(sent, RING, there[k]))  42.4 us
    pallas_call x3, Pallas kernels, attention(): pl.pallas_call(body, grid=(nh,), in_specs=[columns(SEG, 0)] * SLOTS + [co...  33.5 us
    ppermute x12, starting transfers between devices, per_device(): returned[c] = [lax.ppermute(outs[k], RING, back[k]) for k in range(SLOTS)]  26.5 us
    pallas_call x12, Pallas kernels, pack(): pl.pallas_call(body, in_specs=[HBM] * 6 + [ANY] * len(after), out_specs=A...  10.9 us
    ppermute x12, waiting for transfers between devices, per_device(): returned[c] = [lax.ppermute(outs[k], RING, back[k]) for k in range(SLOTS)]  5.63 us
    unnamed x20, local copies, waits for them, and re-layouts  5.11 us
  transfers between devices with their start and end apart: 30, of which 11 were waited for; matrix products, arithmetic and copies ran while one was open for 0% of the time, Pallas kernels for 25%

profile of v2, /device:TPU:1, one launch (start us, length us, event | category | flops | bytes accessed | tf_op | source)
XLA Modules:
  0.0 175.0 jit_solution(6994944426913400025)
XLA Ops:
  0.6 2.2 %pack.12.refs_6_ = bf16[128,3072]{1,0:T(8,128)(2,1)} custom-call(bf16[128,5120]{1,0:T(8,128)(2,1)} %refs_0_.23, bf16[128,5120]{1,0:T(8,128)(2,1)} %refs_1_.23, bf16[128,5120]{1,0:T(8,128)(2,1)} %refs_2_.23, bf16[128,5120]{1,0:T(8,128)(2,1)} %refs_3_.23, bf16[128,5120]{1,0:T(8,128)(2,1)} %refs_4_.23, bf16[128,5120]{1,0:T(8,128)(2,1)} %refs_5_.23), custom_call_target="tpu_custom_call" | custom-call | bytes 1572864 | tf_op jit(solution)/shard_map/pack/pallas_call | solution.py:91
  2.8 4.4 %collective-permute-start = (bf16[128,3072]{1,0:T(8,128)(2,1)}, bf16[128,3072]{1,0:T(8,128)(2,1)}, u32[]{:S(2)}, u32[]{:S(2)}) collective-permute-start(bf16[128,3072]{1,0:T(8,128)(2,1)} %pack.12.refs_6_), channel_id=1, source_target_pairs={{0,1},{1,192},{64,128},{65,193},{128,129},{129,64},{192,0},{193,65... | collective-permute-start | bytes 2359304 | tf_op jit(solution)/shard_map/ppermute | solution.py:264
  7.2 2.1 %pack.13.refs_6_ = bf16[128,3072]{1,0:T(8,128)(2,1)} custom-call(bf16[128,5120]{1,0:T(8,128)(2,1)} %refs_0_.23, bf16[128,5120]{1,0:T(8,128)(2,1)} %refs_1_.23, bf16[128,5120]{1,0:T(8,128)(2,1)} %refs_2_.23, bf16[128,5120]{1,0:T(8,128)(2,1)} %refs_3_.23, bf16[128,5120]{1,0:T(8,128)(2,1)} %refs_4_.23, bf16[128,5120]{1,0:T(8,128)(2,1)} %refs_5_.23, ...), custom_call_target="tpu_custom_call" | custom-call | bytes 1572864 | tf_op jit(solution)/shard_map/pack/pallas_call | solution.py:91
  9.4 2.2 %pack.14.refs_6_ = bf16[128,3072]{1,0:T(8,128)(2,1)} custom-call(bf16[128,5120]{1,0:T(8,128)(2,1)} %refs_0_.23, bf16[128,5120]{1,0:T(8,128)(2,1)} %refs_1_.23, bf16[128,5120]{1,0:T(8,128)(2,1)} %refs_2_.23, bf16[128,5120]{1,0:T(8,128)(2,1)} %refs_3_.23, bf16[128,5120]{1,0:T(8,128)(2,1)} %refs_4_.23, bf16[128,5120]{1,0:T(8,128)(2,1)} %refs_5_.23, ...), custom_call_target="tpu_custom_call" | custom-call | bytes 1572864 | tf_op jit(solution)/shard_map/pack/pallas_call | solution.py:91
  11.7 3.8 %collective-permute-start.2 = (bf16[128,3072]{1,0:T(8,128)(2,1)}, bf16[128,3072]{1,0:T(8,128)(2,1)}, u32[]{:S(2)}, u32[]{:S(2)}) collective-permute-start(bf16[128,3072]{1,0:T(8,128)(2,1)} %pack.14.refs_6_), channel_id=1, source_target_pairs={{0,129},{1,64},{64,0},{65,65},{128,1},{129,192},{192,128},{193,193... | collective-permute-start | bytes 2359304 | tf_op jit(solution)/shard_map/ppermute | solution.py:264
  15.5 2.2 %pack.15.refs_6_ = bf16[128,3072]{1,0:T(8,128)(2,1)} custom-call(bf16[128,5120]{1,0:T(8,128)(2,1)} %refs_0_.23, bf16[128,5120]{1,0:T(8,128)(2,1)} %refs_1_.23, bf16[128,5120]{1,0:T(8,128)(2,1)} %refs_2_.23, bf16[128,5120]{1,0:T(8,128)(2,1)} %refs_3_.23, bf16[128,5120]{1,0:T(8,128)(2,1)} %refs_4_.23, bf16[128,5120]{1,0:T(8,128)(2,1)} %refs_5_.23, ...), custom_call_target="tpu_custom_call" | custom-call | bytes 1572864 | tf_op jit(solution)/shard_map/pack/pallas_call | solution.py:91
  17.7 2.0 %collective-permute-start.3 = (bf16[128,3072]{1,0:T(8,128)(2,1)}, bf16[128,3072]{1,0:T(8,128)(2,1)S(1)}, u32[]{:S(2)}, u32[]{:S(2)}) collective-permute-start(bf16[128,3072]{1,0:T(8,128)(2,1)} %pack.15.refs_6_), channel_id=1, source_target_pairs={{0,0},{1,65},{64,1},{65,192},{128,128},{129,193},{192,129},{193,64... | collective-permute-start | bytes 2359304 | tf_op jit(solution)/shard_map/ppermute | solution.py:264
  19.7 5.2 %collective-permute-done.refs_7_.refs_0_.refs_4_ = bf16[128,3072]{1,0:T(8,128)(2,1)} collective-permute-done((bf16[128,3072]{1,0:T(8,128)(2,1)}, bf16[128,3072]{1,0:T(8,128)(2,1)}, u32[]{:S(2)}, u32[]{:S(2)}) %collective-permute-start) | collective-permute-done | bytes 786464 | tf_op jit(solution)/shard_map/ppermute | solution.py:264
  30.2 4.1 %collective-permute-start.6 = (bf16[128,3072]{1,0:T(8,128)(2,1)S(1)}, bf16[128,3072]{1,0:T(8,128)(2,1)S(1)}, u32[]{:S(2)}, u32[]{:S(2)}) collective-permute-start(bf16[128,3072]{1,0:T(8,128)(2,1)S(1)} %pack.16.refs_6_), channel_id=1, source_target_pairs={{0,1},{1,192},{64,128},{65,193},{128,129},{129,64},{192,0},{193,65... | collective-permute-start | bytes 2359304 | tf_op jit(solution)/shard_map/ppermute | solution.py:264
  34.3 10.1 %collective-permute-done.1.refs_7_.refs_1_.refs_5_ = bf16[128,3072]{1,0:T(8,128)(2,1)} collective-permute-done((bf16[128,3072]{1,0:T(8,128)(2,1)}, bf16[128,3072]{1,0:T(8,128)(2,1)}, u32[]{:S(2)}, u32[]{:S(2)}) %collective-permute-start.1) | collective-permute-done | bytes 786464 | tf_op jit(solution)/shard_map/ppermute | solution.py:264
  46.3 6.7 %collective-permute-done.3.refs_7_.refs_3_ = bf16[128,3072]{1,0:T(8,128)(2,1)S(1)} collective-permute-done((bf16[128,3072]{1,0:T(8,128)(2,1)}, bf16[128,3072]{1,0:T(8,128)(2,1)S(1)}, u32[]{:S(2)}, u32[]{:S(2)}) %collective-permute-start.3) | collective-permute-done | bytes 786464 | tf_op jit(solution)/shard_map/ppermute | solution.py:264
  55.3 4.2 %collective-permute-start.7 = (bf16[128,3072]{1,0:T(8,128)(2,1)S(1)}, bf16[128,3072]{1,0:T(8,128)(2,1)S(1)}, u32[]{:S(2)}, u32[]{:S(2)}) collective-permute-start(bf16[128,3072]{1,0:T(8,128)(2,1)S(1)} %pack.17.refs_6_), channel_id=1, source_target_pairs={{0,128},{1,193},{64,129},{65,64},{128,0},{129,65},{192,1},{193,192... | collective-permute-start | bytes 2359304 | tf_op jit(solution)/shard_map/ppermute | solution.py:264
  59.6 7.3 %collective-permute-start.8 = (bf16[128,3072]{1,0:T(8,128)(2,1)S(1)}, bf16[128,3072]{1,0:T(8,128)(2,1)S(1)}, u32[]{:S(2)}, u32[]{:S(2)}) collective-permute-start(bf16[128,3072]{1,0:T(8,128)(2,1)S(1)} %pack.18.refs_6_), channel_id=1, source_target_pairs={{0,129},{1,64},{64,0},{65,65},{128,1},{129,192},{192,128},{193,193... | collective-permute-start | bytes 2359304 | tf_op jit(solution)/shard_map/ppermute | solution.py:264
  69.2 11.3 %collective-permute-done.7.refs_7_.refs_1_.refs_5_ = bf16[128,3072]{1,0:T(8,128)(2,1)S(1)} collective-permute-done((bf16[128,3072]{1,0:T(8,128)(2,1)S(1)}, bf16[128,3072]{1,0:T(8,128)(2,1)S(1)}, u32[]{:S(2)}, u32[]{:S(2)}) %collective-permute-start.7) | collective-permute-done | bytes 786464 | tf_op jit(solution)/shard_map/ppermute | solution.py:264
  80.8 2.7 %collective-permute-done.8.refs_7_.refs_2_.refs_6_ = bf16[128,3072]{1,0:T(8,128)(2,1)S(1)} collective-permute-done((bf16[128,3072]{1,0:T(8,128)(2,1)S(1)}, bf16[128,3072]{1,0:T(8,128)(2,1)S(1)}, u32[]{:S(2)}, u32[]{:S(2)}) %collective-permute-start.8) | collective-permute-done | bytes 786464 | tf_op jit(solution)/shard_map/ppermute | solution.py:264
  84.6 2.1 %collective-permute-start.14 = (bf16[512,2048]{1,0:T(8,128)(2,1)S(1)}, bf16[512,2048]{1,0:T(8,128)(2,1)S(1)}, u32[]{:S(2)}, u32[]{:S(2)}) collective-permute-start(bf16[512,2048]{1,0:T(8,128)(2,1)S(1)} %join.4.refs_20_.refs_8_.refs_9_.refs_10_.refs_11_), channel_id=1, source_target_pairs={{0,64},{64,0},{1,65},{65,1},{2,66},{66,2},{3,67},{67,3},{4,68},{68... | collective-permute-start | bytes 6291464 | tf_op jit(solution)/shard_map/ppermute | solution.py:275
  86.7 7.4 %collective-permute-start.19 = (bf16[128,1536]{1,0:T(8,128)(2,1)S(1)}, bf16[128,1536]{1,0:T(8,128)(2,1)S(1)}, u32[]{:S(2)}, u32[]{:S(2)}) collective-permute-start(bf16[128,1536]{1,0:T(8,128)(2,1)S(1)} %pack.23.refs_4_), channel_id=1, source_target_pairs={{0,0},{1,65},{64,1},{65,192},{128,128},{129,193},{192,129},{193,64... | collective-permute-start | bytes 1179656 | tf_op jit(solution)/shard_map/ppermute | solution.py:264
  94.1 4.7 %collective-permute-done.19.refs_3_.refs_7_ = bf16[128,1536]{1,0:T(8,128)(2,1)S(1)} collective-permute-done((bf16[128,1536]{1,0:T(8,128)(2,1)S(1)}, bf16[128,1536]{1,0:T(8,128)(2,1)S(1)}, u32[]{:S(2)}, u32[]{:S(2)}) %collective-permute-start.19) | collective-permute-done | bytes 393248 | tf_op jit(solution)/shard_map/ppermute | solution.py:264
  100.7 2.2 %collective-permute-start.17 = (bf16[128,1536]{1,0:T(8,128)(2,1)S(1)}, bf16[128,1536]{1,0:T(8,128)(2,1)S(1)}, u32[]{:S(2)}, u32[]{:S(2)}) collective-permute-start(bf16[128,1536]{1,0:T(8,128)(2,1)S(1)} %pack.21.refs_6_), channel_id=1, source_target_pairs={{0,128},{1,193},{64,129},{65,64},{128,0},{129,65},{192,1},{193,192... | collective-permute-start | bytes 1179656 | tf_op jit(solution)/shard_map/ppermute | solution.py:264
  102.9 3.5 %collective-permute-start.16 = (bf16[128,1536]{1,0:T(8,128)(2,1)S(1)}, bf16[128,1536]{1,0:T(8,128)(2,1)S(1)}, u32[]{:S(2)}, u32[]{:S(2)}) collective-permute-start(bf16[128,1536]{1,0:T(8,128)(2,1)S(1)} %pack.20.refs_6_), channel_id=1, source_target_pairs={{0,1},{1,192},{64,128},{65,193},{128,129},{129,64},{192,0},{193,65... | collective-permute-start | bytes 1179656 | tf_op jit(solution)/shard_map/ppermute | solution.py:264
  106.4 13.3 %attention.3 = (bf16[272,512]{1,0:T(8,128)(2,1)S(1)}, bf16[272,512]{1,0:T(8,128)(2,1)S(1)}, bf16[272,512]{1,0:T(8,128)(2,1)S(1)}, bf16[272,512]{1,0:T(8,128)(2,1)S(1)}) custom-call(bf16[128,3072]{1,0:T(8,128)(2,1)} %collective-permute-done.refs_7_.refs_0_.refs_4_, bf16[128,3072]{1,0:T(8,128)(2,1)} %collective-permute-done.1.refs_7_.refs_1_.refs_5_, ...), custom_call_target="tpu_custom_call" | custom-call | flops 6442450944 | bytes 10000000 | tf_op jit(solution)/shard_map/attention/pallas_call | solution.py:188
  120.9 5.3 %collective-permute-start.10 = (bf16[272,512]{1,0:T(8,128)(2,1)S(1)}, bf16[272,512]{1,0:T(8,128)(2,1)S(1)}, u32[]{:S(2)}, u32[]{:S(2)}) collective-permute-start(bf16[272,512]{1,0:T(8,128)(2,1)S(1)} %get-tuple-element.20.refs_4_), channel_id=1, source_target_pairs={{1,0},{192,1},{128,64},{193,65},{129,128},{64,129},{0,192},{65,193... | collective-permute-start | bytes 835592 | tf_op jit(solution)/shard_map/ppermute | solution.py:279
  126.1 3.3 %collective-permute-start.12 = (bf16[272,512]{1,0:T(8,128)(2,1)S(1)}, bf16[272,512]{1,0:T(8,128)(2,1)S(1)}, u32[]{:S(2)}, u32[]{:S(2)}) collective-permute-start(bf16[272,512]{1,0:T(8,128)(2,1)S(1)} %get-tuple-element.22), channel_id=1, source_target_pairs={{129,0},{64,1},{0,64},{65,65},{1,128},{192,129},{128,192},{193,193... | collective-permute-start | bytes 835592 | tf_op jit(solution)/shard_map/ppermute | solution.py:279
  129.4 13.5 %attention.4 = (bf16[272,512]{1,0:T(8,128)(2,1)S(1)}, bf16[272,512]{1,0:T(8,128)(2,1)S(1)}, bf16[272,512]{1,0:T(8,128)(2,1)S(1)}, bf16[272,512]{1,0:T(8,128)(2,1)S(1)}) custom-call(bf16[128,3072]{1,0:T(8,128)(2,1)S(1)} %collective-permute-done.6.refs_7_.refs_0_.refs_4_, bf16[128,3072]{1,0:T(8,128)(2,1)S(1)} %collective-permute-done.7.refs_7_.refs_1_.refs_5_, ...), custom_call_target="tpu_custom_call" | custom-call | flops 6442450944 | bytes 10000000 | tf_op jit(solution)/shard_map/attention/pallas_call | solution.py:188
  144.9 3.4 %collective-permute-start.20 = (bf16[272,512]{1,0:T(8,128)(2,1)S(1)}, bf16[272,512]{1,0:T(8,128)(2,1)S(1)}, u32[]{:S(2)}, u32[]{:S(2)}) collective-permute-start(bf16[272,512]{1,0:T(8,128)(2,1)S(1)} %get-tuple-element.24.refs_20_), channel_id=1, source_target_pairs={{1,0},{192,1},{128,64},{193,65},{129,128},{64,129},{0,192},{65,193... | collective-permute-start | bytes 835592 | tf_op jit(solution)/shard_map/ppermute | solution.py:279
  148.3 2.1 %collective-permute-start.22 = (bf16[272,512]{1,0:T(8,128)(2,1)S(1)}, bf16[272,512]{1,0:T(8,128)(2,1)S(1)}, u32[]{:S(2)}, u32[]{:S(2)}) collective-permute-start(bf16[272,512]{1,0:T(8,128)(2,1)S(1)} %get-tuple-element.26), channel_id=1, source_target_pairs={{129,0},{64,1},{0,64},{65,65},{1,128},{192,129},{128,192},{193,193... | collective-permute-start | bytes 835592 | tf_op jit(solution)/shard_map/ppermute | solution.py:279
  150.4 2.1 %collective-permute-start.23 = (bf16[272,512]{1,0:T(8,128)(2,1)S(1)}, bf16[272,512]{1,0:T(8,128)(2,1)S(1)}, u32[]{:S(2)}, u32[]{:S(2)}) collective-permute-start(bf16[272,512]{1,0:T(8,128)(2,1)S(1)} %get-tuple-element.27), channel_id=1, source_target_pairs={{0,0},{65,1},{1,64},{192,65},{128,128},{193,129},{129,192},{64,193... | collective-permute-start | bytes 835592 | tf_op jit(solution)/shard_map/ppermute | solution.py:279
  152.5 6.7 %attention.5 = (bf16[272,256]{1,0:T(8,128)(2,1)S(1)}, bf16[272,256]{1,0:T(8,128)(2,1)S(1)}, bf16[272,256]{1,0:T(8,128)(2,1)S(1)}, bf16[272,256]{1,0:T(8,128)(2,1)S(1)}) custom-call(bf16[128,1536]{1,0:T(8,128)(2,1)S(1)} %collective-permute-done.16.refs_0_.refs_4_, bf16[128,1536]{1,0:T(8,128)(2,1)S(1)} %collective-permute-done.17.refs_1_.refs_5_, ...), custom_call_target="tpu_custom_call" | custom-call | flops 3221225472 | bytes 5000000 | tf_op jit(solution)/shard_map/attention/pallas_call | solution.py:188
  159.3 4.6 %collective-permute-start.26 = (bf16[272,256]{1,0:T(8,128)(2,1)S(1)}, bf16[272,256]{1,0:T(8,128)(2,1)S(1)}, u32[]{:S(2)}, u32[]{:S(2)}) collective-permute-start(bf16[272,256]{1,0:T(8,128)(2,1)S(1)} %get-tuple-element.28), channel_id=1, source_target_pairs={{1,0},{192,1},{128,64},{193,65},{129,128},{64,129},{0,192},{65,193... | collective-permute-start | bytes 417800 | tf_op jit(solution)/shard_map/ppermute | solution.py:279
  165.8 1.9 %collective-permute-start.29 = (bf16[272,256]{1,0:T(8,128)(2,1)S(1)}, bf16[272,256]{1,0:T(8,128)(2,1)S(1)}, u32[]{:S(2)}, u32[]{:S(2)}) collective-permute-start(bf16[272,256]{1,0:T(8,128)(2,1)S(1)} %get-tuple-element.31), channel_id=1, source_target_pairs={{0,0},{65,1},{1,64},{192,65},{128,128},{193,129},{129,192},{64,193... | collective-permute-start | bytes 417800 | tf_op jit(solution)/shard_map/ppermute | solution.py:279
  168.3 2.8 %collective-permute-done.27.refs_9_ = bf16[272,256]{1,0:T(8,128)(2,1)S(1)} collective-permute-done((bf16[272,256]{1,0:T(8,128)(2,1)S(1)}, bf16[272,256]{1,0:T(8,128)(2,1)S(1)}, u32[]{:S(2)}, u32[]{:S(2)}) %collective-permute-start.27) | collective-permute-done | bytes 139296 | tf_op jit(solution)/shard_map/ppermute | solution.py:279
  171.1 2.3 %collective-permute-done.29.refs_11_ = bf16[272,256]{1,0:T(8,128)(2,1)S(1)} collective-permute-done((bf16[272,256]{1,0:T(8,128)(2,1)S(1)}, bf16[272,256]{1,0:T(8,128)(2,1)S(1)}, u32[]{:S(2)}, u32[]{:S(2)}) %collective-permute-start.29) | collective-permute-done | bytes 139296 | tf_op jit(solution)/shard_map/ppermute | solution.py:279
  (67 shorter events, 22.4 us)
Async XLA Ops:
  2.8 22.0 %collective-permute-start = (bf16[128,3072]{1,0:T(8,128)(2,1)}, bf16[128,3072]{1,0:T(8,128)(2,1)}, u32[]{:S(2)}, u32[]{:S(2)}) collective-permute-start(bf16[128,3072]{1,0:T(8,128)(2,1)} %pack.12.refs_6_), channel_id=1, source_target_pairs={{0,1},{1,192},{64,128},{65,193},{128,129},{129,64},{192,0},{193,65... | collective-permute-start | bytes 2359304 | tf_op jit(solution)/shard_map/ppermute | solution.py:264
  9.3 35.0 %collective-permute-start.1 = (bf16[128,3072]{1,0:T(8,128)(2,1)}, bf16[128,3072]{1,0:T(8,128)(2,1)}, u32[]{:S(2)}, u32[]{:S(2)}) collective-permute-start(bf16[128,3072]{1,0:T(8,128)(2,1)} %pack.13.refs_6_), channel_id=1, source_target_pairs={{0,128},{1,193},{64,129},{65,64},{128,0},{129,65},{192,1},{193,192... | collective-permute-start | bytes 2359304 | tf_op jit(solution)/shard_map/ppermute | solution.py:264
  11.7 34.4 %collective-permute-start.2 = (bf16[128,3072]{1,0:T(8,128)(2,1)}, bf16[128,3072]{1,0:T(8,128)(2,1)}, u32[]{:S(2)}, u32[]{:S(2)}) collective-permute-start(bf16[128,3072]{1,0:T(8,128)(2,1)} %pack.14.refs_6_), channel_id=1, source_target_pairs={{0,129},{1,64},{64,0},{65,65},{128,1},{129,192},{192,128},{193,193... | collective-permute-start | bytes 2359304 | tf_op jit(solution)/shard_map/ppermute | solution.py:264
  17.7 35.3 %collective-permute-start.3 = (bf16[128,3072]{1,0:T(8,128)(2,1)}, bf16[128,3072]{1,0:T(8,128)(2,1)S(1)}, u32[]{:S(2)}, u32[]{:S(2)}) collective-permute-start(bf16[128,3072]{1,0:T(8,128)(2,1)} %pack.15.refs_6_), channel_id=1, source_target_pairs={{0,0},{1,65},{64,1},{65,192},{128,128},{129,193},{192,129},{193,64... | collective-permute-start | bytes 2359304 | tf_op jit(solution)/shard_map/ppermute | solution.py:264
  30.2 36.7 %collective-permute-start.6 = (bf16[128,3072]{1,0:T(8,128)(2,1)S(1)}, bf16[128,3072]{1,0:T(8,128)(2,1)S(1)}, u32[]{:S(2)}, u32[]{:S(2)}) collective-permute-start(bf16[128,3072]{1,0:T(8,128)(2,1)S(1)} %pack.16.refs_6_), channel_id=1, source_target_pairs={{0,1},{1,192},{64,128},{65,193},{128,129},{129,64},{192,0},{193,65... | collective-permute-start | bytes 2359304 | tf_op jit(solution)/shard_map/ppermute | solution.py:264
  53.2 15.6 %copy-start.4 = (bf16[128,5120]{1,0:T(8,128)(2,1)S(1)}, bf16[128,5120]{1,0:T(8,128)(2,1)}, u32[]{:S(2)}) copy-start(bf16[128,5120]{1,0:T(8,128)(2,1)} %refs_3_.23) | copy-start | bytes 3932164
  53.2 15.6 %copy-start.6 = (bf16[128,5120]{1,0:T(8,128)(2,1)S(1)}, bf16[128,5120]{1,0:T(8,128)(2,1)}, u32[]{:S(2)}) copy-start(bf16[128,5120]{1,0:T(8,128)(2,1)} %refs_4_.23) | copy-start | bytes 3932164
  55.1 45.6 %collective-permute-start.4 = (bf16[512,2048]{1,0:T(8,128)(2,1)S(1)}, bf16[512,2048]{1,0:T(8,128)(2,1)S(1)}, u32[]{:S(2)}, u32[]{:S(2)}) collective-permute-start(bf16[512,2048]{1,0:T(8,128)(2,1)S(1)} %join.3.refs_6_.refs_8_.refs_9_.refs_10_.refs_11_), channel_id=1, source_target_pairs={{0,64},{64,0},{1,65},{65,1},{2,66},{66,2},{3,67},{67,3},{4,68},{68... | collective-permute-start | bytes 6291464 | tf_op jit(solution)/shard_map/ppermute | solution.py:275
  55.2 47.7 %collective-permute-start.5 = (bf16[512,2048]{1,0:T(8,128)(2,1)S(1)}, bf16[512,2048]{1,0:T(8,128)(2,1)S(1)}, u32[]{:S(2)}, u32[]{:S(2)}) collective-permute-start(bf16[512,2048]{1,0:T(8,128)(2,1)S(1)} %join.3.refs_6_.refs_8_.refs_9_.refs_10_.refs_11_), channel_id=1, source_target_pairs={{64,2},{66,4},{68,6},{70,8},{72,10},{74,12},{76,14},{78,16},{80,18... | collective-permute-start | bytes 6291464 | tf_op jit(solution)/shard_map/ppermute | solution.py:271
  55.3 25.1 %collective-permute-start.7 = (bf16[128,3072]{1,0:T(8,128)(2,1)S(1)}, bf16[128,3072]{1,0:T(8,128)(2,1)S(1)}, u32[]{:S(2)}, u32[]{:S(2)}) collective-permute-start(bf16[128,3072]{1,0:T(8,128)(2,1)S(1)} %pack.17.refs_6_), channel_id=1, source_target_pairs={{0,128},{1,193},{64,129},{65,64},{128,0},{129,65},{192,1},{193,192... | collective-permute-start | bytes 2359304 | tf_op jit(solution)/shard_map/ppermute | solution.py:264
  59.6 23.9 %collective-permute-start.8 = (bf16[128,3072]{1,0:T(8,128)(2,1)S(1)}, bf16[128,3072]{1,0:T(8,128)(2,1)S(1)}, u32[]{:S(2)}, u32[]{:S(2)}) collective-permute-start(bf16[128,3072]{1,0:T(8,128)(2,1)S(1)} %pack.18.refs_6_), channel_id=1, source_target_pairs={{0,129},{1,64},{64,0},{65,65},{128,1},{129,192},{192,128},{193,193... | collective-permute-start | bytes 2359304 | tf_op jit(solution)/shard_map/ppermute | solution.py:264
  66.9 17.3 %collective-permute-start.9 = (bf16[128,3072]{1,0:T(8,128)(2,1)S(1)}, bf16[128,3072]{1,0:T(8,128)(2,1)S(1)}, u32[]{:S(2)}, u32[]{:S(2)}) collective-permute-start(bf16[128,3072]{1,0:T(8,128)(2,1)S(1)} %pack.19.refs_4_), channel_id=1, source_target_pairs={{0,0},{1,65},{64,1},{65,192},{128,128},{129,193},{192,129},{193,64... | collective-permute-start | bytes 2359304 | tf_op jit(solution)/shard_map/ppermute | solution.py:264
  84.6 41.5 %collective-permute-start.14 = (bf16[512,2048]{1,0:T(8,128)(2,1)S(1)}, bf16[512,2048]{1,0:T(8,128)(2,1)S(1)}, u32[]{:S(2)}, u32[]{:S(2)}) collective-permute-start(bf16[512,2048]{1,0:T(8,128)(2,1)S(1)} %join.4.refs_20_.refs_8_.refs_9_.refs_10_.refs_11_), channel_id=1, source_target_pairs={{0,64},{64,0},{1,65},{65,1},{2,66},{66,2},{3,67},{67,3},{4,68},{68... | collective-permute-start | bytes 6291464 | tf_op jit(solution)/shard_map/ppermute | solution.py:275
  86.7 39.5 %collective-permute-start.15 = (bf16[512,2048]{1,0:T(8,128)(2,1)S(1)}, bf16[512,2048]{1,0:T(8,128)(2,1)S(1)}, u32[]{:S(2)}, u32[]{:S(2)}) collective-permute-start(bf16[512,2048]{1,0:T(8,128)(2,1)S(1)} %join.4.refs_20_.refs_8_.refs_9_.refs_10_.refs_11_), channel_id=1, source_target_pairs={{64,2},{66,4},{68,6},{70,8},{72,10},{74,12},{76,14},{78,16},{80,18... | collective-permute-start | bytes 6291464 | tf_op jit(solution)/shard_map/ppermute | solution.py:271
  86.7 12.1 %collective-permute-start.19 = (bf16[128,1536]{1,0:T(8,128)(2,1)S(1)}, bf16[128,1536]{1,0:T(8,128)(2,1)S(1)}, u32[]{:S(2)}, u32[]{:S(2)}) collective-permute-start(bf16[128,1536]{1,0:T(8,128)(2,1)S(1)} %pack.23.refs_4_), channel_id=1, source_target_pairs={{0,0},{1,65},{64,1},{65,192},{128,128},{129,193},{192,129},{193,64... | collective-permute-start | bytes 1179656 | tf_op jit(solution)/shard_map/ppermute | solution.py:264
  98.8 20.9 %collective-permute-start.18 = (bf16[128,1536]{1,0:T(8,128)(2,1)S(1)}, bf16[128,1536]{1,0:T(8,128)(2,1)S(1)}, u32[]{:S(2)}, u32[]{:S(2)}) collective-permute-start(bf16[128,1536]{1,0:T(8,128)(2,1)S(1)} %pack.22.refs_6_), channel_id=1, source_target_pairs={{0,129},{1,64},{64,0},{65,65},{128,1},{129,192},{192,128},{193,193... | collective-permute-start | bytes 1179656 | tf_op jit(solution)/shard_map/ppermute | solution.py:264
  100.7 19.1 %collective-permute-start.17 = (bf16[128,1536]{1,0:T(8,128)(2,1)S(1)}, bf16[128,1536]{1,0:T(8,128)(2,1)S(1)}, u32[]{:S(2)}, u32[]{:S(2)}) collective-permute-start(bf16[128,1536]{1,0:T(8,128)(2,1)S(1)} %pack.21.refs_6_), channel_id=1, source_target_pairs={{0,128},{1,193},{64,129},{65,64},{128,0},{129,65},{192,1},{193,192... | collective-permute-start | bytes 1179656 | tf_op jit(solution)/shard_map/ppermute | solution.py:264
  102.9 16.9 %collective-permute-start.16 = (bf16[128,1536]{1,0:T(8,128)(2,1)S(1)}, bf16[128,1536]{1,0:T(8,128)(2,1)S(1)}, u32[]{:S(2)}, u32[]{:S(2)}) collective-permute-start(bf16[128,1536]{1,0:T(8,128)(2,1)S(1)} %pack.20.refs_6_), channel_id=1, source_target_pairs={{0,1},{1,192},{64,128},{65,193},{128,129},{129,64},{192,0},{193,65... | collective-permute-start | bytes 1179656 | tf_op jit(solution)/shard_map/ppermute | solution.py:264
  119.8 28.4 %collective-permute-start.24 = (bf16[512,1024]{1,0:T(8,128)(2,1)S(1)}, bf16[512,1024]{1,0:T(8,128)(2,1)S(1)}, u32[]{:S(2)}, u32[]{:S(2)}) collective-permute-start(bf16[512,1024]{1,0:T(8,128)(2,1)S(1)} %join.5.refs_20_.refs_8_.refs_9_.refs_10_.refs_11_), channel_id=1, source_target_pairs={{0,64},{64,0},{1,65},{65,1},{2,66},{66,2},{3,67},{67,3},{4,68},{68... | collective-permute-start | bytes 3145736 | tf_op jit(solution)/shard_map/ppermute | solution.py:275
  120.9 29.5 %collective-permute-start.25 = (bf16[512,1024]{1,0:T(8,128)(2,1)S(1)}, bf16[512,1024]{1,0:T(8,128)(2,1)S(1)}, u32[]{:S(2)}, u32[]{:S(2)}) collective-permute-start(bf16[512,1024]{1,0:T(8,128)(2,1)S(1)} %join.5.refs_20_.refs_8_.refs_9_.refs_10_.refs_11_), channel_id=1, source_target_pairs={{64,2},{66,4},{68,6},{70,8},{72,10},{74,12},{76,14},{78,16},{80,18... | collective-permute-start | bytes 3145736 | tf_op jit(solution)/shard_map/ppermute | solution.py:271
  120.9 22.1 %collective-permute-start.10 = (bf16[272,512]{1,0:T(8,128)(2,1)S(1)}, bf16[272,512]{1,0:T(8,128)(2,1)S(1)}, u32[]{:S(2)}, u32[]{:S(2)}) collective-permute-start(bf16[272,512]{1,0:T(8,128)(2,1)S(1)} %get-tuple-element.20.refs_4_), channel_id=1, source_target_pairs={{1,0},{192,1},{128,64},{193,65},{129,128},{64,129},{0,192},{65,193... | collective-permute-start | bytes 835592 | tf_op jit(solution)/shard_map/ppermute | solution.py:279
  126.1 18.8 %collective-permute-start.11 = (bf16[272,512]{1,0:T(8,128)(2,1)S(1)}, bf16[272,512]{1,0:T(8,128)(2,1)S(1)}, u32[]{:S(2)}, u32[]{:S(2)}) collective-permute-start(bf16[272,512]{1,0:T(8,128)(2,1)S(1)} %get-tuple-element.21), channel_id=1, source_target_pairs={{128,0},{193,1},{129,64},{64,65},{0,128},{65,129},{1,192},{192,193... | collective-permute-start | bytes 835592 | tf_op jit(solution)/shard_map/ppermute | solution.py:279
  126.1 22.1 %collective-permute-start.12 = (bf16[272,512]{1,0:T(8,128)(2,1)S(1)}, bf16[272,512]{1,0:T(8,128)(2,1)S(1)}, u32[]{:S(2)}, u32[]{:S(2)}) collective-permute-start(bf16[272,512]{1,0:T(8,128)(2,1)S(1)} %get-tuple-element.22), channel_id=1, source_target_pairs={{129,0},{64,1},{0,64},{65,65},{1,128},{192,129},{128,192},{193,193... | collective-permute-start | bytes 835592 | tf_op jit(solution)/shard_map/ppermute | solution.py:279
  142.9 16.3 %collective-permute-start.13 = (bf16[272,512]{1,0:T(8,128)(2,1)S(1)}, bf16[272,512]{1,0:T(8,128)(2,1)S(1)}, u32[]{:S(2)}, u32[]{:S(2)}) collective-permute-start(bf16[272,512]{1,0:T(8,128)(2,1)S(1)} %get-tuple-element.23), channel_id=1, source_target_pairs={{0,0},{65,1},{1,64},{192,65},{128,128},{193,129},{129,192},{64,193... | collective-permute-start | bytes 835592 | tf_op jit(solution)/shard_map/ppermute | solution.py:279
  144.9 19.0 %collective-permute-start.20 = (bf16[272,512]{1,0:T(8,128)(2,1)S(1)}, bf16[272,512]{1,0:T(8,128)(2,1)S(1)}, u32[]{:S(2)}, u32[]{:S(2)}) collective-permute-start(bf16[272,512]{1,0:T(8,128)(2,1)S(1)} %get-tuple-element.24.refs_20_), channel_id=1, source_target_pairs={{1,0},{192,1},{128,64},{193,65},{129,128},{64,129},{0,192},{65,193... | collective-permute-start | bytes 835592 | tf_op jit(solution)/shard_map/ppermute | solution.py:279
  148.3 15.6 %collective-permute-start.21 = (bf16[272,512]{1,0:T(8,128)(2,1)S(1)}, bf16[272,512]{1,0:T(8,128)(2,1)S(1)}, u32[]{:S(2)}, u32[]{:S(2)}) collective-permute-start(bf16[272,512]{1,0:T(8,128)(2,1)S(1)} %get-tuple-element.25), channel_id=1, source_target_pairs={{128,0},{193,1},{129,64},{64,65},{0,128},{65,129},{1,192},{192,193... | collective-permute-start | bytes 835592 | tf_op jit(solution)/shard_map/ppermute | solution.py:279
  148.3 17.5 %collective-permute-start.22 = (bf16[272,512]{1,0:T(8,128)(2,1)S(1)}, bf16[272,512]{1,0:T(8,128)(2,1)S(1)}, u32[]{:S(2)}, u32[]{:S(2)}) collective-permute-start(bf16[272,512]{1,0:T(8,128)(2,1)S(1)} %get-tuple-element.26), channel_id=1, source_target_pairs={{129,0},{64,1},{0,64},{65,65},{1,128},{192,129},{128,192},{193,193... | collective-permute-start | bytes 835592 | tf_op jit(solution)/shard_map/ppermute | solution.py:279
  150.4 17.4 %collective-permute-start.23 = (bf16[272,512]{1,0:T(8,128)(2,1)S(1)}, bf16[272,512]{1,0:T(8,128)(2,1)S(1)}, u32[]{:S(2)}, u32[]{:S(2)}) collective-permute-start(bf16[272,512]{1,0:T(8,128)(2,1)S(1)} %get-tuple-element.27), channel_id=1, source_target_pairs={{0,0},{65,1},{1,64},{192,65},{128,128},{193,129},{129,192},{64,193... | collective-permute-start | bytes 835592 | tf_op jit(solution)/shard_map/ppermute | solution.py:279
  159.3 9.0 %collective-permute-start.26 = (bf16[272,256]{1,0:T(8,128)(2,1)S(1)}, bf16[272,256]{1,0:T(8,128)(2,1)S(1)}, u32[]{:S(2)}, u32[]{:S(2)}) collective-permute-start(bf16[272,256]{1,0:T(8,128)(2,1)S(1)} %get-tuple-element.28), channel_id=1, source_target_pairs={{1,0},{192,1},{128,64},{193,65},{129,128},{64,129},{0,192},{65,193... | collective-permute-start | bytes 417800 | tf_op jit(solution)/shard_map/ppermute | solution.py:279
  163.9 7.2 %collective-permute-start.27 = (bf16[272,256]{1,0:T(8,128)(2,1)S(1)}, bf16[272,256]{1,0:T(8,128)(2,1)S(1)}, u32[]{:S(2)}, u32[]{:S(2)}) collective-permute-start(bf16[272,256]{1,0:T(8,128)(2,1)S(1)} %get-tuple-element.29), channel_id=1, source_target_pairs={{128,0},{193,1},{129,64},{64,65},{0,128},{65,129},{1,192},{192,193... | collective-permute-start | bytes 417800 | tf_op jit(solution)/shard_map/ppermute | solution.py:279
  163.9 7.2 %collective-permute-start.28 = (bf16[272,256]{1,0:T(8,128)(2,1)S(1)}, bf16[272,256]{1,0:T(8,128)(2,1)S(1)}, u32[]{:S(2)}, u32[]{:S(2)}) collective-permute-start(bf16[272,256]{1,0:T(8,128)(2,1)S(1)} %get-tuple-element.30), channel_id=1, source_target_pairs={{129,0},{64,1},{0,64},{65,65},{1,128},{192,129},{128,192},{193,193... | collective-permute-start | bytes 417800 | tf_op jit(solution)/shard_map/ppermute | solution.py:279
  165.8 7.6 %collective-permute-start.29 = (bf16[272,256]{1,0:T(8,128)(2,1)S(1)}, bf16[272,256]{1,0:T(8,128)(2,1)S(1)}, u32[]{:S(2)}, u32[]{:S(2)}) collective-permute-start(bf16[272,256]{1,0:T(8,128)(2,1)S(1)} %get-tuple-element.31), channel_id=1, source_target_pairs={{0,0},{65,1},{1,64},{192,65},{128,128},{193,129},{129,192},{64,193... | collective-permute-start | bytes 417800 | tf_op jit(solution)/shard_map/ppermute | solution.py:279
  (8 other events, 60.3 us)

commit v3 on v2

--- a/solution.py
+++ b/solution.py
@@ -11,6 +11,7 @@
 SEG = 128
 BLK = 512
 ROWS = 256
+PAIR = 2
 SLOTS = 4
 OUT_ROWS = 2 * SEG + 16
 SCALE = 1.0 / DH**0.5
@@ -21,26 +22,25 @@
 STEPS = ((1, 2, 3, 0), (2, 3, 0, 1))
 CHUNKS = (4, 4, 2)
 WINDOW = 4
-GATHER = False
 ORDER = (
-    ("pack", 0),
-    ("pack", 0),
-    ("pack", 0),
-    ("pack", 0),
-    ("pack", 0),
-    ("pack", 0),
-    ("pack", 0),
-    ("pack", 0),
-    ("join", 0),
-    ("pack", 0),
-    ("pack", 0),
-    ("pack", 0),
-    ("pack", 0),
-    ("join", 1),
-    ("attend", 0),
-    ("join", 2),
-    ("attend", 1),
-    ("attend", 2),
+    ("pack", 0, ()),
+    ("pack", 0, ()),
+    ("pack", 0, ()),
+    ("pack", 0, ()),
+    ("pack", 1, ()),
+    ("pack", 1, ()),
+    ("pack", 1, ()),
+    ("pack", 1, ()),
+    ("join", 0, ()),
+    ("pack", 2, ()),
+    ("pack", 2, ()),
+    ("pack", 2, ()),
+    ("pack", 2, ()),
+    ("join", 1, ()),
+    ("attend", 0, ()),
+    ("join", 2, (1,)),
+    ("attend", 1, ()),
+    ("attend", 2, ()),
 )
 ANY = pl.BlockSpec(memory_space=pl.ANY)
 HBM = pl.BlockSpec(memory_space=pltpu.HBM)
@@ -123,29 +123,34 @@
     )(*messages, *after)
 
 
-def attend_rows(plain_q, joined_q, key_refs):
+def score_rows(plain_q, joined_q, key_refs, cols):
     nt = (((1,), (1,)), ((), ()))
     scores, tangents = [], []
     for k, dk, v, dv in key_refs:
-        plain_k = k[...]
-        joined_k = jnp.concatenate([plain_k, dk[...]], axis=1)
+        plain_k = k[:, cols]
+        joined_k = jnp.concatenate([plain_k, dk[:, cols]], axis=1)
         scores.append(lax.dot_general(plain_q, plain_k, nt, preferred_element_type=jnp.float32))
         tangents.append(lax.dot_general(joined_q, joined_k, nt, preferred_element_type=jnp.float32))
+    return scores, tangents
+
+
+def weigh_rows(scores, tangents, key_refs, cols):
     top = functools.reduce(jnp.maximum, [jnp.max(s, axis=-1, keepdims=True) for s in scores])
     expo = [jnp.exp2((s - top) * (SCALE * LOG2E)) for s in scores]
     total = sum(jnp.sum(e, axis=-1, keepdims=True) for e in expo)
-    mean = sum(jnp.sum(e * t, axis=-1, keepdims=True) for e, t in zip(expo, tangents)) / total
+    inverse = 1.0 / total
+    mean = sum(jnp.sum(e * t, axis=-1, keepdims=True) for e, t in zip(expo, tangents)) * inverse
     both = jnp.zeros((ROWS, 2 * DH), jnp.float32)
     slope = jnp.zeros((ROWS, DH), jnp.float32)
     for (k, dk, v, dv), e, t in zip(key_refs, expo, tangents):
-        low = e.astype(jnp.bfloat16)
-        tan_low = (e * (t - mean)).astype(jnp.bfloat16)
-        joined_v = jnp.concatenate([v[...], dv[...]], axis=1)
+        probs = e * inverse
+        low = probs.astype(jnp.bfloat16)
+        tan_low = (probs * (t - mean)).astype(jnp.bfloat16)
+        joined_v = jnp.concatenate([v[:, cols], dv[:, cols]], axis=1)
         both = both + jnp.dot(low, joined_v, preferred_element_type=jnp.float32)
-        slope = slope + jnp.dot(tan_low, v[...], preferred_element_type=jnp.float32)
-    inverse = 1.0 / total
-    attended = both[:, :DH] * inverse
-    attended_tan = (both[:, DH:] + slope * SCALE) * inverse
+        slope = slope + jnp.dot(tan_low, v[:, cols], preferred_element_type=jnp.float32)
+    attended = both[:, :DH]
+    attended_tan = both[:, DH:] + slope * SCALE
     log_total = top * SCALE + jnp.log(total)
     log_total_tan = mean * SCALE
     return attended, attended_tan, log_total, log_total_tan
@@ -165,36 +170,47 @@
         key_refs = [refs[4 * i : 4 * i + 4] for i in range(len(keysets))]
         outs = refs[4 * len(keysets) + len(after) :]
         per = ROWS // SEG
-        for part in range(BLK // ROWS):
+        units = [(j, part) for j in range(PAIR) for part in range(BLK // ROWS)]
+
+        def products(j, part):
+            cols = slice(j * DH, (j + 1) * DH)
             here = range(part * per, part * per + per)
-            plain_q = jnp.concatenate([q_refs[k][...] for k in here], axis=0)
-            tan_q = jnp.concatenate([tan_refs[k][...] for k in here], axis=0)
-            joined_q = jnp.concatenate([tan_q, plain_q], axis=1)
-            attended, attended_tan, log_total, log_total_tan = attend_rows(plain_q, joined_q, key_refs)
+            plain_q = jnp.concatenate([q_refs[k][:, cols] for k in here], axis=0)
+            tan_q = jnp.concatenate([tan_refs[k][:, cols] for k in here], axis=0)
+            return score_rows(plain_q, jnp.concatenate([tan_q, plain_q], axis=1), key_refs, cols)
+
+        ready = products(*units[0])
+        for u, (j, part) in enumerate(units):
+            cols = slice(j * DH, (j + 1) * DH)
+            held = ready
+            if u + 1 < len(units):
+                ready = products(*units[u + 1])
+            attended, attended_tan, log_total, log_total_tan = weigh_rows(*held, key_refs, cols)
             lane = lax.broadcasted_iota(jnp.int32, (ROWS, DH), 1)
             stats = jnp.where(lane == 0, log_total, jnp.where(lane == 1, log_total_tan, 0.0))
             pieces = [piece.astype(jnp.float32) for piece in split3(stats)]
-            for s, k in enumerate(here):
+            for s in range(per):
+                k = part * per + s
                 rows = slice(s * SEG, (s + 1) * SEG)
-                outs[k][0:SEG, :] = attended[rows].astype(jnp.bfloat16)
-                outs[k][SEG : 2 * SEG, :] = attended_tan[rows].astype(jnp.bfloat16)
+                outs[k][0:SEG, cols] = attended[rows].astype(jnp.bfloat16)
+                outs[k][SEG : 2 * SEG, cols] = attended_tan[rows].astype(jnp.bfloat16)
                 lines = [piece[rows].T[0:2] for piece in pieces]
                 lines.append(jnp.zeros((10, SEG), jnp.float32))
-                outs[k][2 * SEG : OUT_ROWS, :] = jnp.concatenate(lines, axis=0).astype(jnp.bfloat16)
+                outs[k][2 * SEG : OUT_ROWS, cols] = jnp.concatenate(lines, axis=0).astype(jnp.bfloat16)
 
     def columns(rows, i):
-        return pl.BlockSpec((rows, DH), lambda h: (0, i * nh + h))
+        return pl.BlockSpec((rows, PAIR * DH), lambda h: (0, i * (nh // PAIR) + h))
 
     return pl.pallas_call(
         body,
-        grid=(nh,),
+        grid=(nh // PAIR,),
         in_specs=[columns(SEG, 0)] * SLOTS
         + [columns(SEG, 1)] * SLOTS
         + [columns(keyset.shape[0], i) for keyset in keysets for i in range(4)]
         + [ANY] * len(after),
         out_specs=[columns(OUT_ROWS, 0)] * SLOTS,
         out_shape=[jax.ShapeDtypeStruct((OUT_ROWS, nh * DH), jnp.bfloat16)] * SLOTS,
-        compiler_params=pltpu.CompilerParams(vmem_limit_bytes=20 * MIB),
+        compiler_params=pltpu.CompilerParams(vmem_limit_bytes=28 * MIB),
         cost_estimate=pl.CostEstimate(
             flops=nh * 2 * 16 * BLK * 3 * BLK * DH // 2,
             bytes_accessed=nh * 2_500_000,
@@ -255,7 +271,8 @@
     n = len(plan)
     arrived, joined, others, returned = [], [None] * n, [None] * n, [None] * n
     last = []
-    for kind, c in ORDER:
+    for kind, c, seen in ORDER:
+        last = last + [array for i in seen for array in others[i][1:]]
         if kind == "pack":
             m, k = len(arrived), len(arrived) % SLOTS
             base, nh = plan[m // SLOTS]
@@ -269,10 +286,7 @@
         if kind == "join":
             joined[c] = join(messages, nh, last)
             outer = lax.ppermute(joined[c], LINE, outer_pairs(length))
-            if GATHER:
-                others[c] = (lax.all_gather(joined[c], "core", axis=0, tiled=True), outer)
-            else:
-                others[c] = (joined[c], lax.ppermute(joined[c], "core", [(0, 1), (1, 0)]), outer)
+            others[c] = (joined[c], lax.ppermute(joined[c], "core", [(0, 1), (1, 0)]), outer)
             last = [joined[c]]
         else:
             outs = attention(messages, others[c], nh, last)

time: 176 us -> 166 us (0.943)
  Pallas kernels: 48.1 us -> 40.4 us
  starting transfers between devices: 72.6 us -> 66.8 us
  waiting for transfers between devices: 48 us -> 51.8 us
    pallas_call x3, Pallas kernels: 33.5 us -> 25.9 us  [attention(): pl.pallas_call(body, grid=(nh // PAIR,), in_specs=[columns(SEG, 0)] * SLO...]
    ppermute x12, starting transfers between devices: 42.8 us -> 37.9 us  [per_device(): arrived.append(lax.ppermute(sent, RING, there[k]))]
    ppermute x12, waiting for transfers between devices: 42.4 us -> 47.1 us  [per_device(): arrived.append(lax.ppermute(sent, RING, there[k]))]
    ppermute x3, starting transfers between devices: 3.19 us -> 1.17 us  [per_device(): lax.ppermute(joined[c], 'core', [(0, 1), (1, 0)])]
  transfers between devices with their start and end apart: 30 -> 30, of which waited for: 11 -> 11; matrix products, arithmetic and copies ran while one was open for 0% -> 0% of each run, Pallas kernels for 25% -> 22%
where the time goes in v3:
time: 166 us; the launch traced here: 165 us
  starting transfers between devices  66.8 us (40%)
  waiting for transfers between devices  51.8 us (31%)
  Pallas kernels  40.4 us (24%)
  local copies, waits for them, and re-layouts  5.11 us (3%)
    ppermute x12, waiting for transfers between devices, per_device(): arrived.append(lax.ppermute(sent, RING, there[k]))  47.1 us
    ppermute x12, starting transfers between devices, per_device(): arrived.append(lax.ppermute(sent, RING, there[k]))  37.9 us
    ppermute x12, starting transfers between devices, per_device(): returned[c] = [lax.ppermute(outs[k], RING, back[k]) for k in range(SLOTS)]  27.7 us
    pallas_call x3, Pallas kernels, attention(): pl.pallas_call(body, grid=(nh // PAIR,), in_specs=[columns(SEG, 0)] * SLO...  25.9 us
    pallas_call x12, Pallas kernels, pack(): pl.pallas_call(body, in_specs=[HBM] * 6 + [ANY] * len(after), out_specs=A...  10.9 us
    unnamed x20, local copies, waits for them, and re-layouts  5.11 us
    ppermute x12, waiting for transfers between devices, per_device(): returned[c] = [lax.ppermute(outs[k], RING, back[k]) for k in range(SLOTS)]  4.68 us
  transfers between devices with their start and end apart: 30, of which 11 were waited for; matrix products, arithmetic and copies ran while one was open for 0% of the time, Pallas kernels for 22%

profile of v3, /device:TPU:1, one launch (start us, length us, event | category | flops | bytes accessed | tf_op | source)
XLA Modules:
  0.0 165.2 jit_solution(6675420778027840060)
XLA Ops:
  0.6 2.2 %pack.12.refs_6_ = bf16[128,3072]{1,0:T(8,128)(2,1)} custom-call(bf16[128,5120]{1,0:T(8,128)(2,1)} %refs_0_.23, bf16[128,5120]{1,0:T(8,128)(2,1)} %refs_1_.23, bf16[128,5120]{1,0:T(8,128)(2,1)} %refs_2_.23, bf16[128,5120]{1,0:T(8,128)(2,1)} %refs_3_.23, bf16[128,5120]{1,0:T(8,128)(2,1)} %refs_4_.23, bf16[128,5120]{1,0:T(8,128)(2,1)} %refs_5_.23), custom_call_target="tpu_custom_call" | custom-call | bytes 1572864 | tf_op jit(solution)/shard_map/pack/pallas_call | solution.py:91
  2.8 4.4 %collective-permute-start = (bf16[128,3072]{1,0:T(8,128)(2,1)}, bf16[128,3072]{1,0:T(8,128)(2,1)}, u32[]{:S(2)}, u32[]{:S(2)}) collective-permute-start(bf16[128,3072]{1,0:T(8,128)(2,1)} %pack.12.refs_6_), channel_id=1, source_target_pairs={{0,1},{1,192},{64,128},{65,193},{128,129},{129,64},{192,0},{193,65... | collective-permute-start | bytes 2359304 | tf_op jit(solution)/shard_map/ppermute | solution.py:281
  7.2 2.1 %pack.13.refs_6_ = bf16[128,3072]{1,0:T(8,128)(2,1)} custom-call(bf16[128,5120]{1,0:T(8,128)(2,1)} %refs_0_.23, bf16[128,5120]{1,0:T(8,128)(2,1)} %refs_1_.23, bf16[128,5120]{1,0:T(8,128)(2,1)} %refs_2_.23, bf16[128,5120]{1,0:T(8,128)(2,1)} %refs_3_.23, bf16[128,5120]{1,0:T(8,128)(2,1)} %refs_4_.23, bf16[128,5120]{1,0:T(8,128)(2,1)} %refs_5_.23, ...), custom_call_target="tpu_custom_call" | custom-call | bytes 1572864 | tf_op jit(solution)/shard_map/pack/pallas_call | solution.py:91
  9.4 2.2 %pack.14.refs_6_ = bf16[128,3072]{1,0:T(8,128)(2,1)} custom-call(bf16[128,5120]{1,0:T(8,128)(2,1)} %refs_0_.23, bf16[128,5120]{1,0:T(8,128)(2,1)} %refs_1_.23, bf16[128,5120]{1,0:T(8,128)(2,1)} %refs_2_.23, bf16[128,5120]{1,0:T(8,128)(2,1)} %refs_3_.23, bf16[128,5120]{1,0:T(8,128)(2,1)} %refs_4_.23, bf16[128,5120]{1,0:T(8,128)(2,1)} %refs_5_.23, ...), custom_call_target="tpu_custom_call" | custom-call | bytes 1572864 | tf_op jit(solution)/shard_map/pack/pallas_call | solution.py:91
  11.7 3.8 %collective-permute-start.2 = (bf16[128,3072]{1,0:T(8,128)(2,1)}, bf16[128,3072]{1,0:T(8,128)(2,1)}, u32[]{:S(2)}, u32[]{:S(2)}) collective-permute-start(bf16[128,3072]{1,0:T(8,128)(2,1)} %pack.14.refs_6_), channel_id=1, source_target_pairs={{0,129},{1,64},{64,0},{65,65},{128,1},{129,192},{192,128},{193,193... | collective-permute-start | bytes 2359304 | tf_op jit(solution)/shard_map/ppermute | solution.py:281
  15.5 2.2 %pack.15.refs_6_ = bf16[128,3072]{1,0:T(8,128)(2,1)} custom-call(bf16[128,5120]{1,0:T(8,128)(2,1)} %refs_0_.23, bf16[128,5120]{1,0:T(8,128)(2,1)} %refs_1_.23, bf16[128,5120]{1,0:T(8,128)(2,1)} %refs_2_.23, bf16[128,5120]{1,0:T(8,128)(2,1)} %refs_3_.23, bf16[128,5120]{1,0:T(8,128)(2,1)} %refs_4_.23, bf16[128,5120]{1,0:T(8,128)(2,1)} %refs_5_.23, ...), custom_call_target="tpu_custom_call" | custom-call | bytes 1572864 | tf_op jit(solution)/shard_map/pack/pallas_call | solution.py:91
  17.7 2.0 %collective-permute-start.3 = (bf16[128,3072]{1,0:T(8,128)(2,1)}, bf16[128,3072]{1,0:T(8,128)(2,1)S(1)}, u32[]{:S(2)}, u32[]{:S(2)}) collective-permute-start(bf16[128,3072]{1,0:T(8,128)(2,1)} %pack.15.refs_6_), channel_id=1, source_target_pairs={{0,0},{1,65},{64,1},{65,192},{128,128},{129,193},{192,129},{193,64... | collective-permute-start | bytes 2359304 | tf_op jit(solution)/shard_map/ppermute | solution.py:281
  19.7 5.2 %collective-permute-done.refs_7_.refs_0_.refs_4_ = bf16[128,3072]{1,0:T(8,128)(2,1)} collective-permute-done((bf16[128,3072]{1,0:T(8,128)(2,1)}, bf16[128,3072]{1,0:T(8,128)(2,1)}, u32[]{:S(2)}, u32[]{:S(2)}) %collective-permute-start) | collective-permute-done | bytes 786464 | tf_op jit(solution)/shard_map/ppermute | solution.py:281
  30.2 4.1 %collective-permute-start.6 = (bf16[128,3072]{1,0:T(8,128)(2,1)S(1)}, bf16[128,3072]{1,0:T(8,128)(2,1)S(1)}, u32[]{:S(2)}, u32[]{:S(2)}) collective-permute-start(bf16[128,3072]{1,0:T(8,128)(2,1)S(1)} %pack.16.refs_6_), channel_id=1, source_target_pairs={{0,1},{1,192},{64,128},{65,193},{128,129},{129,64},{192,0},{193,65... | collective-permute-start | bytes 2359304 | tf_op jit(solution)/shard_map/ppermute | solution.py:281
  34.3 10.1 %collective-permute-done.1.refs_7_.refs_1_.refs_5_ = bf16[128,3072]{1,0:T(8,128)(2,1)} collective-permute-done((bf16[128,3072]{1,0:T(8,128)(2,1)}, bf16[128,3072]{1,0:T(8,128)(2,1)}, u32[]{:S(2)}, u32[]{:S(2)}) %collective-permute-start.1) | collective-permute-done | bytes 786464 | tf_op jit(solution)/shard_map/ppermute | solution.py:281
  44.6 4.3 %collective-permute-start.7 = (bf16[128,3072]{1,0:T(8,128)(2,1)S(1)}, bf16[128,3072]{1,0:T(8,128)(2,1)S(1)}, u32[]{:S(2)}, u32[]{:S(2)}) collective-permute-start(bf16[128,3072]{1,0:T(8,128)(2,1)S(1)} %pack.17.refs_6_), channel_id=1, source_target_pairs={{0,128},{1,193},{64,129},{65,64},{128,0},{129,65},{192,1},{193,192... | collective-permute-start | bytes 2359304 | tf_op jit(solution)/shard_map/ppermute | solution.py:281
  49.1 1.9 %collective-permute-start.8 = (bf16[128,3072]{1,0:T(8,128)(2,1)S(1)}, bf16[128,3072]{1,0:T(8,128)(2,1)S(1)}, u32[]{:S(2)}, u32[]{:S(2)}) collective-permute-start(bf16[128,3072]{1,0:T(8,128)(2,1)S(1)} %pack.18.refs_6_), channel_id=1, source_target_pairs={{0,129},{1,64},{64,0},{65,65},{128,1},{129,192},{192,128},{193,193... | collective-permute-start | bytes 2359304 | tf_op jit(solution)/shard_map/ppermute | solution.py:281
  53.2 2.2 %collective-permute-start.9 = (bf16[128,3072]{1,0:T(8,128)(2,1)S(1)}, bf16[128,3072]{1,0:T(8,128)(2,1)S(1)}, u32[]{:S(2)}, u32[]{:S(2)}) collective-permute-start(bf16[128,3072]{1,0:T(8,128)(2,1)S(1)} %pack.19.refs_4_), channel_id=1, source_target_pairs={{0,0},{1,65},{64,1},{65,192},{128,128},{129,193},{192,129},{193,64... | collective-permute-start | bytes 2359304 | tf_op jit(solution)/shard_map/ppermute | solution.py:281
  57.3 4.8 %collective-permute-done.6.refs_7_.refs_0_.refs_4_ = bf16[128,3072]{1,0:T(8,128)(2,1)S(1)} collective-permute-done((bf16[128,3072]{1,0:T(8,128)(2,1)S(1)}, bf16[128,3072]{1,0:T(8,128)(2,1)S(1)}, u32[]{:S(2)}, u32[]{:S(2)}) %collective-permute-start.6) | collective-permute-done | bytes 786464 | tf_op jit(solution)/shard_map/ppermute | solution.py:281
  62.5 11.4 %collective-permute-done.7.refs_7_.refs_1_.refs_5_ = bf16[128,3072]{1,0:T(8,128)(2,1)S(1)} collective-permute-done((bf16[128,3072]{1,0:T(8,128)(2,1)S(1)}, bf16[128,3072]{1,0:T(8,128)(2,1)S(1)}, u32[]{:S(2)}, u32[]{:S(2)}) %collective-permute-start.7) | collective-permute-done | bytes 786464 | tf_op jit(solution)/shard_map/ppermute | solution.py:281
  79.1 7.6 %collective-permute-start.16 = (bf16[128,1536]{1,0:T(8,128)(2,1)S(1)}, bf16[128,1536]{1,0:T(8,128)(2,1)S(1)}, u32[]{:S(2)}, u32[]{:S(2)}) collective-permute-start(bf16[128,1536]{1,0:T(8,128)(2,1)S(1)} %pack.20.refs_6_), channel_id=1, source_target_pairs={{0,1},{1,192},{64,128},{65,193},{128,129},{129,64},{192,0},{193,65... | collective-permute-start | bytes 1179656 | tf_op jit(solution)/shard_map/ppermute | solution.py:281
  86.7 10.6 %collective-permute-done.16.refs_0_.refs_4_ = bf16[128,1536]{1,0:T(8,128)(2,1)S(1)} collective-permute-done((bf16[128,1536]{1,0:T(8,128)(2,1)S(1)}, bf16[128,1536]{1,0:T(8,128)(2,1)S(1)}, u32[]{:S(2)}, u32[]{:S(2)}) %collective-permute-start.16) | collective-permute-done | bytes 393248 | tf_op jit(solution)/shard_map/ppermute | solution.py:281
  99.1 2.7 %collective-permute-start.18 = (bf16[128,1536]{1,0:T(8,128)(2,1)S(1)}, bf16[128,1536]{1,0:T(8,128)(2,1)S(1)}, u32[]{:S(2)}, u32[]{:S(2)}) collective-permute-start(bf16[128,1536]{1,0:T(8,128)(2,1)S(1)} %pack.22.refs_6_), channel_id=1, source_target_pairs={{0,129},{1,64},{64,0},{65,65},{128,1},{129,192},{192,128},{193,193... | collective-permute-start | bytes 1179656 | tf_op jit(solution)/shard_map/ppermute | solution.py:281
  101.8 3.0 %collective-permute-start.19 = (bf16[128,1536]{1,0:T(8,128)(2,1)S(1)}, bf16[128,1536]{1,0:T(8,128)(2,1)S(1)}, u32[]{:S(2)}, u32[]{:S(2)}) collective-permute-start(bf16[128,1536]{1,0:T(8,128)(2,1)S(1)} %pack.23.refs_4_), channel_id=1, source_target_pairs={{0,0},{1,65},{64,1},{65,192},{128,128},{129,193},{192,129},{193,64... | collective-permute-start | bytes 1179656 | tf_op jit(solution)/shard_map/ppermute | solution.py:281
  104.9 10.5 %attention.3 = (bf16[272,512]{1,0:T(8,128)(2,1)S(1)}, bf16[272,512]{1,0:T(8,128)(2,1)S(1)}, bf16[272,512]{1,0:T(8,128)(2,1)S(1)}, bf16[272,512]{1,0:T(8,128)(2,1)S(1)}) custom-call(bf16[128,3072]{1,0:T(8,128)(2,1)} %collective-permute-done.refs_7_.refs_0_.refs_4_, bf16[128,3072]{1,0:T(8,128)(2,1)} %collective-permute-done.1.refs_7_.refs_1_.refs_5_, ...), custom_call_target="tpu_custom_call" | custom-call | flops 6442450944 | bytes 10000000 | tf_op jit(solution)/shard_map/attention/pallas_call | solution.py:204
  115.7 2.5 %collective-permute-start.10 = (bf16[272,512]{1,0:T(8,128)(2,1)S(1)}, bf16[272,512]{1,0:T(8,128)(2,1)S(1)}, u32[]{:S(2)}, u32[]{:S(2)}) collective-permute-start(bf16[272,512]{1,0:T(8,128)(2,1)S(1)} %get-tuple-element.20.refs_4_), channel_id=1, source_target_pairs={{1,0},{192,1},{128,64},{193,65},{129,128},{64,129},{0,192},{65,193... | collective-permute-start | bytes 835592 | tf_op jit(solution)/shard_map/ppermute | solution.py:293
  118.3 6.2 %collective-permute-start.12 = (bf16[272,512]{1,0:T(8,128)(2,1)S(1)}, bf16[272,512]{1,0:T(8,128)(2,1)S(1)}, u32[]{:S(2)}, u32[]{:S(2)}) collective-permute-start(bf16[272,512]{1,0:T(8,128)(2,1)S(1)} %get-tuple-element.22), channel_id=1, source_target_pairs={{129,0},{64,1},{0,64},{65,65},{1,128},{192,129},{128,192},{193,193... | collective-permute-start | bytes 835592 | tf_op jit(solution)/shard_map/ppermute | solution.py:293
  124.5 10.6 %attention.4 = (bf16[272,512]{1,0:T(8,128)(2,1)S(1)}, bf16[272,512]{1,0:T(8,128)(2,1)S(1)}, bf16[272,512]{1,0:T(8,128)(2,1)S(1)}, bf16[272,512]{1,0:T(8,128)(2,1)S(1)}) custom-call(bf16[128,3072]{1,0:T(8,128)(2,1)S(1)} %collective-permute-done.6.refs_7_.refs_0_.refs_4_, bf16[128,3072]{1,0:T(8,128)(2,1)S(1)} %collective-permute-done.7.refs_7_.refs_1_.refs_5_, ...), custom_call_target="tpu_custom_call" | custom-call | flops 6442450944 | bytes 10000000 | tf_op jit(solution)/shard_map/attention/pallas_call | solution.py:204
  135.1 3.1 %collective-permute-start.13 = (bf16[272,512]{1,0:T(8,128)(2,1)S(1)}, bf16[272,512]{1,0:T(8,128)(2,1)S(1)}, u32[]{:S(2)}, u32[]{:S(2)}) collective-permute-start(bf16[272,512]{1,0:T(8,128)(2,1)S(1)} %get-tuple-element.23), channel_id=1, source_target_pairs={{0,0},{65,1},{1,64},{192,65},{128,128},{193,129},{129,192},{64,193... | collective-permute-start | bytes 835592 | tf_op jit(solution)/shard_map/ppermute | solution.py:293
  138.2 2.2 %collective-permute-start.20 = (bf16[272,512]{1,0:T(8,128)(2,1)S(1)}, bf16[272,512]{1,0:T(8,128)(2,1)S(1)}, u32[]{:S(2)}, u32[]{:S(2)}) collective-permute-start(bf16[272,512]{1,0:T(8,128)(2,1)S(1)} %get-tuple-element.24.refs_20_), channel_id=1, source_target_pairs={{1,0},{192,1},{128,64},{193,65},{129,128},{64,129},{0,192},{65,193... | collective-permute-start | bytes 835592 | tf_op jit(solution)/shard_map/ppermute | solution.py:293
  143.0 2.2 %collective-permute-start.23 = (bf16[272,512]{1,0:T(8,128)(2,1)S(1)}, bf16[272,512]{1,0:T(8,128)(2,1)S(1)}, u32[]{:S(2)}, u32[]{:S(2)}) collective-permute-start(bf16[272,512]{1,0:T(8,128)(2,1)S(1)} %get-tuple-element.27), channel_id=1, source_target_pairs={{0,0},{65,1},{1,64},{192,65},{128,128},{193,129},{129,192},{64,193... | collective-permute-start | bytes 835592 | tf_op jit(solution)/shard_map/ppermute | solution.py:293
  145.2 4.8 %attention.5 = (bf16[272,256]{1,0:T(8,128)(2,1)S(1)}, bf16[272,256]{1,0:T(8,128)(2,1)S(1)}, bf16[272,256]{1,0:T(8,128)(2,1)S(1)}, bf16[272,256]{1,0:T(8,128)(2,1)S(1)}) custom-call(bf16[128,1536]{1,0:T(8,128)(2,1)S(1)} %collective-permute-done.16.refs_0_.refs_4_, bf16[128,1536]{1,0:T(8,128)(2,1)S(1)} %collective-permute-done.17.refs_1_.refs_5_, ...), custom_call_target="tpu_custom_call" | custom-call | flops 3221225472 | bytes 5000000 | tf_op jit(solution)/shard_map/attention/pallas_call | solution.py:204
  150.0 4.1 %collective-permute-start.26 = (bf16[272,256]{1,0:T(8,128)(2,1)S(1)}, bf16[272,256]{1,0:T(8,128)(2,1)S(1)}, u32[]{:S(2)}, u32[]{:S(2)}) collective-permute-start(bf16[272,256]{1,0:T(8,128)(2,1)S(1)} %get-tuple-element.28), channel_id=1, source_target_pairs={{1,0},{192,1},{128,64},{193,65},{129,128},{64,129},{0,192},{65,193... | collective-permute-start | bytes 417800 | tf_op jit(solution)/shard_map/ppermute | solution.py:293
  154.5 2.5 %collective-permute-start.28 = (bf16[272,256]{1,0:T(8,128)(2,1)S(1)}, bf16[272,256]{1,0:T(8,128)(2,1)S(1)}, u32[]{:S(2)}, u32[]{:S(2)}) collective-permute-start(bf16[272,256]{1,0:T(8,128)(2,1)S(1)} %get-tuple-element.30), channel_id=1, source_target_pairs={{129,0},{64,1},{0,64},{65,65},{1,128},{192,129},{128,192},{193,193... | collective-permute-start | bytes 417800 | tf_op jit(solution)/shard_map/ppermute | solution.py:293
  157.0 1.9 %collective-permute-start.29 = (bf16[272,256]{1,0:T(8,128)(2,1)S(1)}, bf16[272,256]{1,0:T(8,128)(2,1)S(1)}, u32[]{:S(2)}, u32[]{:S(2)}) collective-permute-start(bf16[272,256]{1,0:T(8,128)(2,1)S(1)} %get-tuple-element.31), channel_id=1, source_target_pairs={{0,0},{65,1},{1,64},{192,65},{128,128},{193,129},{129,192},{64,193... | collective-permute-start | bytes 417800 | tf_op jit(solution)/shard_map/ppermute | solution.py:293
  159.1 2.2 %collective-permute-done.27.refs_9_ = bf16[272,256]{1,0:T(8,128)(2,1)S(1)} collective-permute-done((bf16[272,256]{1,0:T(8,128)(2,1)S(1)}, bf16[272,256]{1,0:T(8,128)(2,1)S(1)}, u32[]{:S(2)}, u32[]{:S(2)}) %collective-permute-start.27) | collective-permute-done | bytes 139296 | tf_op jit(solution)/shard_map/ppermute | solution.py:293
  161.3 2.3 %collective-permute-done.29.refs_11_ = bf16[272,256]{1,0:T(8,128)(2,1)S(1)} collective-permute-done((bf16[272,256]{1,0:T(8,128)(2,1)S(1)}, bf16[272,256]{1,0:T(8,128)(2,1)S(1)}, u32[]{:S(2)}, u32[]{:S(2)}) %collective-permute-start.29) | collective-permute-done | bytes 139296 | tf_op jit(solution)/shard_map/ppermute | solution.py:293
  (67 shorter events, 22.2 us)
Async XLA Ops:
  2.8 22.0 %collective-permute-start = (bf16[128,3072]{1,0:T(8,128)(2,1)}, bf16[128,3072]{1,0:T(8,128)(2,1)}, u32[]{:S(2)}, u32[]{:S(2)}) collective-permute-start(bf16[128,3072]{1,0:T(8,128)(2,1)} %pack.12.refs_6_), channel_id=1, source_target_pairs={{0,1},{1,192},{64,128},{65,193},{128,129},{129,64},{192,0},{193,65... | collective-permute-start | bytes 2359304 | tf_op jit(solution)/shard_map/ppermute | solution.py:281
  9.3 35.0 %collective-permute-start.1 = (bf16[128,3072]{1,0:T(8,128)(2,1)}, bf16[128,3072]{1,0:T(8,128)(2,1)}, u32[]{:S(2)}, u32[]{:S(2)}) collective-permute-start(bf16[128,3072]{1,0:T(8,128)(2,1)} %pack.13.refs_6_), channel_id=1, source_target_pairs={{0,128},{1,193},{64,129},{65,64},{128,0},{129,65},{192,1},{193,192... | collective-permute-start | bytes 2359304 | tf_op jit(solution)/shard_map/ppermute | solution.py:281
  11.6 13.2 %copy-start = (bf16[128,5120]{1,0:T(8,128)(2,1)S(1)}, bf16[128,5120]{1,0:T(8,128)(2,1)}, u32[]{:S(2)}) copy-start(bf16[128,5120]{1,0:T(8,128)(2,1)} %refs_0_.23) | copy-start | bytes 3932164
  11.7 13.2 %copy-start.1 = (bf16[128,5120]{1,0:T(8,128)(2,1)S(1)}, bf16[128,5120]{1,0:T(8,128)(2,1)}, u32[]{:S(2)}) copy-start(bf16[128,5120]{1,0:T(8,128)(2,1)} %refs_1_.23) | copy-start | bytes 3932164
  11.7 37.2 %collective-permute-start.2 = (bf16[128,3072]{1,0:T(8,128)(2,1)}, bf16[128,3072]{1,0:T(8,128)(2,1)}, u32[]{:S(2)}, u32[]{:S(2)}) collective-permute-start(bf16[128,3072]{1,0:T(8,128)(2,1)} %pack.14.refs_6_), channel_id=1, source_target_pairs={{0,129},{1,64},{64,0},{65,65},{128,1},{129,192},{192,128},{193,193... | collective-permute-start | bytes 2359304 | tf_op jit(solution)/shard_map/ppermute | solution.py:281
  17.7 35.3 %collective-permute-start.3 = (bf16[128,3072]{1,0:T(8,128)(2,1)}, bf16[128,3072]{1,0:T(8,128)(2,1)S(1)}, u32[]{:S(2)}, u32[]{:S(2)}) collective-permute-start(bf16[128,3072]{1,0:T(8,128)(2,1)} %pack.15.refs_6_), channel_id=1, source_target_pairs={{0,0},{1,65},{64,1},{65,192},{128,128},{129,193},{192,129},{193,64... | collective-permute-start | bytes 2359304 | tf_op jit(solution)/shard_map/ppermute | solution.py:281
  30.2 31.9 %collective-permute-start.6 = (bf16[128,3072]{1,0:T(8,128)(2,1)S(1)}, bf16[128,3072]{1,0:T(8,128)(2,1)S(1)}, u32[]{:S(2)}, u32[]{:S(2)}) collective-permute-start(bf16[128,3072]{1,0:T(8,128)(2,1)S(1)} %pack.16.refs_6_), channel_id=1, source_target_pairs={{0,1},{1,192},{64,128},{65,193},{128,129},{129,64},{192,0},{193,65... | collective-permute-start | bytes 2359304 | tf_op jit(solution)/shard_map/ppermute | solution.py:281
  44.6 29.3 %collective-permute-start.7 = (bf16[128,3072]{1,0:T(8,128)(2,1)S(1)}, bf16[128,3072]{1,0:T(8,128)(2,1)S(1)}, u32[]{:S(2)}, u32[]{:S(2)}) collective-permute-start(bf16[128,3072]{1,0:T(8,128)(2,1)S(1)} %pack.17.refs_6_), channel_id=1, source_target_pairs={{0,128},{1,193},{64,129},{65,64},{128,0},{129,65},{192,1},{193,192... | collective-permute-start | bytes 2359304 | tf_op jit(solution)/shard_map/ppermute | solution.py:281
  49.1 26.8 %collective-permute-start.8 = (bf16[128,3072]{1,0:T(8,128)(2,1)S(1)}, bf16[128,3072]{1,0:T(8,128)(2,1)S(1)}, u32[]{:S(2)}, u32[]{:S(2)}) collective-permute-start(bf16[128,3072]{1,0:T(8,128)(2,1)S(1)} %pack.18.refs_6_), channel_id=1, source_target_pairs={{0,129},{1,64},{64,0},{65,65},{128,1},{129,192},{192,128},{193,193... | collective-permute-start | bytes 2359304 | tf_op jit(solution)/shard_map/ppermute | solution.py:281
  53.2 24.4 %collective-permute-start.9 = (bf16[128,3072]{1,0:T(8,128)(2,1)S(1)}, bf16[128,3072]{1,0:T(8,128)(2,1)S(1)}, u32[]{:S(2)}, u32[]{:S(2)}) collective-permute-start(bf16[128,3072]{1,0:T(8,128)(2,1)S(1)} %pack.19.refs_4_), channel_id=1, source_target_pairs={{0,0},{1,65},{64,1},{65,192},{128,128},{129,193},{192,129},{193,64... | collective-permute-start | bytes 2359304 | tf_op jit(solution)/shard_map/ppermute | solution.py:281
  57.2 41.9 %collective-permute-start.4 = (bf16[512,2048]{1,0:T(8,128)(2,1)S(1)}, bf16[512,2048]{1,0:T(8,128)(2,1)S(1)}, u32[]{:S(2)}, u32[]{:S(2)}) collective-permute-start(bf16[512,2048]{1,0:T(8,128)(2,1)S(1)} %join.3.refs_6_.refs_8_.refs_9_.refs_10_.refs_11_), channel_id=1, source_target_pairs={{0,64},{64,0},{1,65},{65,1},{2,66},{66,2},{3,67},{67,3},{4,68},{68... | collective-permute-start | bytes 6291464 | tf_op jit(solution)/shard_map/ppermute | solution.py:289
  62.1 39.7 %collective-permute-start.5 = (bf16[512,2048]{1,0:T(8,128)(2,1)S(1)}, bf16[512,2048]{1,0:T(8,128)(2,1)S(1)}, u32[]{:S(2)}, u32[]{:S(2)}) collective-permute-start(bf16[512,2048]{1,0:T(8,128)(2,1)S(1)} %join.3.refs_6_.refs_8_.refs_9_.refs_10_.refs_11_), channel_id=1, source_target_pairs={{64,2},{66,4},{68,6},{70,8},{72,10},{74,12},{76,14},{78,16},{80,18... | collective-permute-start | bytes 6291464 | tf_op jit(solution)/shard_map/ppermute | solution.py:288
  78.1 37.3 %collective-permute-start.14 = (bf16[512,2048]{1,0:T(8,128)(2,1)S(1)}, bf16[512,2048]{1,0:T(8,128)(2,1)S(1)}, u32[]{:S(2)}, u32[]{:S(2)}) collective-permute-start(bf16[512,2048]{1,0:T(8,128)(2,1)S(1)} %join.4.refs_20_.refs_8_.refs_9_.refs_10_.refs_11_), channel_id=1, source_target_pairs={{0,64},{64,0},{1,65},{65,1},{2,66},{66,2},{3,67},{67,3},{4,68},{68... | collective-permute-start | bytes 6291464 | tf_op jit(solution)/shard_map/ppermute | solution.py:289
  79.1 36.3 %collective-permute-start.15 = (bf16[512,2048]{1,0:T(8,128)(2,1)S(1)}, bf16[512,2048]{1,0:T(8,128)(2,1)S(1)}, u32[]{:S(2)}, u32[]{:S(2)}) collective-permute-start(bf16[512,2048]{1,0:T(8,128)(2,1)S(1)} %join.4.refs_20_.refs_8_.refs_9_.refs_10_.refs_11_), channel_id=1, source_target_pairs={{64,2},{66,4},{68,6},{70,8},{72,10},{74,12},{76,14},{78,16},{80,18... | collective-permute-start | bytes 6291464 | tf_op jit(solution)/shard_map/ppermute | solution.py:288
  79.1 18.2 %collective-permute-start.16 = (bf16[128,1536]{1,0:T(8,128)(2,1)S(1)}, bf16[128,1536]{1,0:T(8,128)(2,1)S(1)}, u32[]{:S(2)}, u32[]{:S(2)}) collective-permute-start(bf16[128,1536]{1,0:T(8,128)(2,1)S(1)} %pack.20.refs_6_), channel_id=1, source_target_pairs={{0,1},{1,192},{64,128},{65,193},{128,129},{129,64},{192,0},{193,65... | collective-permute-start | bytes 1179656 | tf_op jit(solution)/shard_map/ppermute | solution.py:281
  97.3 18.1 %collective-permute-start.17 = (bf16[128,1536]{1,0:T(8,128)(2,1)S(1)}, bf16[128,1536]{1,0:T(8,128)(2,1)S(1)}, u32[]{:S(2)}, u32[]{:S(2)}) collective-permute-start(bf16[128,1536]{1,0:T(8,128)(2,1)S(1)} %pack.21.refs_6_), channel_id=1, source_target_pairs={{0,128},{1,193},{64,129},{65,64},{128,0},{129,65},{192,1},{193,192... | collective-permute-start | bytes 1179656 | tf_op jit(solution)/shard_map/ppermute | solution.py:281
  99.1 16.3 %collective-permute-start.18 = (bf16[128,1536]{1,0:T(8,128)(2,1)S(1)}, bf16[128,1536]{1,0:T(8,128)(2,1)S(1)}, u32[]{:S(2)}, u32[]{:S(2)}) collective-permute-start(bf16[128,1536]{1,0:T(8,128)(2,1)S(1)} %pack.22.refs_6_), channel_id=1, source_target_pairs={{0,129},{1,64},{64,0},{65,65},{128,1},{129,192},{192,128},{193,193... | collective-permute-start | bytes 1179656 | tf_op jit(solution)/shard_map/ppermute | solution.py:281
  101.8 13.6 %collective-permute-start.19 = (bf16[128,1536]{1,0:T(8,128)(2,1)S(1)}, bf16[128,1536]{1,0:T(8,128)(2,1)S(1)}, u32[]{:S(2)}, u32[]{:S(2)}) collective-permute-start(bf16[128,1536]{1,0:T(8,128)(2,1)S(1)} %pack.23.refs_4_), channel_id=1, source_target_pairs={{0,0},{1,65},{64,1},{65,192},{128,128},{129,193},{192,129},{193,64... | collective-permute-start | bytes 1179656 | tf_op jit(solution)/shard_map/ppermute | solution.py:281
  115.5 25.6 %collective-permute-start.24 = (bf16[512,1024]{1,0:T(8,128)(2,1)S(1)}, bf16[512,1024]{1,0:T(8,128)(2,1)S(1)}, u32[]{:S(2)}, u32[]{:S(2)}) collective-permute-start(bf16[512,1024]{1,0:T(8,128)(2,1)S(1)} %join.5.refs_20_.refs_8_.refs_9_.refs_10_.refs_11_), channel_id=1, source_target_pairs={{0,64},{64,0},{1,65},{65,1},{2,66},{66,2},{3,67},{67,3},{4,68},{68... | collective-permute-start | bytes 3145736 | tf_op jit(solution)/shard_map/ppermute | solution.py:289
  115.6 27.4 %collective-permute-start.25 = (bf16[512,1024]{1,0:T(8,128)(2,1)S(1)}, bf16[512,1024]{1,0:T(8,128)(2,1)S(1)}, u32[]{:S(2)}, u32[]{:S(2)}) collective-permute-start(bf16[512,1024]{1,0:T(8,128)(2,1)S(1)} %join.5.refs_20_.refs_8_.refs_9_.refs_10_.refs_11_), channel_id=1, source_target_pairs={{64,2},{66,4},{68,6},{70,8},{72,10},{74,12},{76,14},{78,16},{80,18... | collective-permute-start | bytes 3145736 | tf_op jit(solution)/shard_map/ppermute | solution.py:288
  115.7 19.4 %collective-permute-start.10 = (bf16[272,512]{1,0:T(8,128)(2,1)S(1)}, bf16[272,512]{1,0:T(8,128)(2,1)S(1)}, u32[]{:S(2)}, u32[]{:S(2)}) collective-permute-start(bf16[272,512]{1,0:T(8,128)(2,1)S(1)} %get-tuple-element.20.refs_4_), channel_id=1, source_target_pairs={{1,0},{192,1},{128,64},{193,65},{129,128},{64,129},{0,192},{65,193... | collective-permute-start | bytes 835592 | tf_op jit(solution)/shard_map/ppermute | solution.py:293
  118.3 20.0 %collective-permute-start.11 = (bf16[272,512]{1,0:T(8,128)(2,1)S(1)}, bf16[272,512]{1,0:T(8,128)(2,1)S(1)}, u32[]{:S(2)}, u32[]{:S(2)}) collective-permute-start(bf16[272,512]{1,0:T(8,128)(2,1)S(1)} %get-tuple-element.21), channel_id=1, source_target_pairs={{128,0},{193,1},{129,64},{64,65},{0,128},{65,129},{1,192},{192,193... | collective-permute-start | bytes 835592 | tf_op jit(solution)/shard_map/ppermute | solution.py:293
  118.3 22.1 %collective-permute-start.12 = (bf16[272,512]{1,0:T(8,128)(2,1)S(1)}, bf16[272,512]{1,0:T(8,128)(2,1)S(1)}, u32[]{:S(2)}, u32[]{:S(2)}) collective-permute-start(bf16[272,512]{1,0:T(8,128)(2,1)S(1)} %get-tuple-element.22), channel_id=1, source_target_pairs={{129,0},{64,1},{0,64},{65,65},{1,128},{192,129},{128,192},{193,193... | collective-permute-start | bytes 835592 | tf_op jit(solution)/shard_map/ppermute | solution.py:293
  135.1 14.9 %collective-permute-start.13 = (bf16[272,512]{1,0:T(8,128)(2,1)S(1)}, bf16[272,512]{1,0:T(8,128)(2,1)S(1)}, u32[]{:S(2)}, u32[]{:S(2)}) collective-permute-start(bf16[272,512]{1,0:T(8,128)(2,1)S(1)} %get-tuple-element.23), channel_id=1, source_target_pairs={{0,0},{65,1},{1,64},{192,65},{128,128},{193,129},{129,192},{64,193... | collective-permute-start | bytes 835592 | tf_op jit(solution)/shard_map/ppermute | solution.py:293
  138.2 15.9 %collective-permute-start.20 = (bf16[272,512]{1,0:T(8,128)(2,1)S(1)}, bf16[272,512]{1,0:T(8,128)(2,1)S(1)}, u32[]{:S(2)}, u32[]{:S(2)}) collective-permute-start(bf16[272,512]{1,0:T(8,128)(2,1)S(1)} %get-tuple-element.24.refs_20_), channel_id=1, source_target_pairs={{1,0},{192,1},{128,64},{193,65},{129,128},{64,129},{0,192},{65,193... | collective-permute-start | bytes 835592 | tf_op jit(solution)/shard_map/ppermute | solution.py:293
  140.4 14.1 %collective-permute-start.21 = (bf16[272,512]{1,0:T(8,128)(2,1)S(1)}, bf16[272,512]{1,0:T(8,128)(2,1)S(1)}, u32[]{:S(2)}, u32[]{:S(2)}) collective-permute-start(bf16[272,512]{1,0:T(8,128)(2,1)S(1)} %get-tuple-element.25), channel_id=1, source_target_pairs={{128,0},{193,1},{129,64},{64,65},{0,128},{65,129},{1,192},{192,193... | collective-permute-start | bytes 835592 | tf_op jit(solution)/shard_map/ppermute | solution.py:293
  141.1 15.9 %collective-permute-start.22 = (bf16[272,512]{1,0:T(8,128)(2,1)S(1)}, bf16[272,512]{1,0:T(8,128)(2,1)S(1)}, u32[]{:S(2)}, u32[]{:S(2)}) collective-permute-start(bf16[272,512]{1,0:T(8,128)(2,1)S(1)} %get-tuple-element.26), channel_id=1, source_target_pairs={{129,0},{64,1},{0,64},{65,65},{1,128},{192,129},{128,192},{193,193... | collective-permute-start | bytes 835592 | tf_op jit(solution)/shard_map/ppermute | solution.py:293
  143.0 15.9 %collective-permute-start.23 = (bf16[272,512]{1,0:T(8,128)(2,1)S(1)}, bf16[272,512]{1,0:T(8,128)(2,1)S(1)}, u32[]{:S(2)}, u32[]{:S(2)}) collective-permute-start(bf16[272,512]{1,0:T(8,128)(2,1)S(1)} %get-tuple-element.27), channel_id=1, source_target_pairs={{0,0},{65,1},{1,64},{192,65},{128,128},{193,129},{129,192},{64,193... | collective-permute-start | bytes 835592 | tf_op jit(solution)/shard_map/ppermute | solution.py:293
  150.0 9.1 %collective-permute-start.26 = (bf16[272,256]{1,0:T(8,128)(2,1)S(1)}, bf16[272,256]{1,0:T(8,128)(2,1)S(1)}, u32[]{:S(2)}, u32[]{:S(2)}) collective-permute-start(bf16[272,256]{1,0:T(8,128)(2,1)S(1)} %get-tuple-element.28), channel_id=1, source_target_pairs={{1,0},{192,1},{128,64},{193,65},{129,128},{64,129},{0,192},{65,193... | collective-permute-start | bytes 417800 | tf_op jit(solution)/shard_map/ppermute | solution.py:293
  154.1 7.2 %collective-permute-start.27 = (bf16[272,256]{1,0:T(8,128)(2,1)S(1)}, bf16[272,256]{1,0:T(8,128)(2,1)S(1)}, u32[]{:S(2)}, u32[]{:S(2)}) collective-permute-start(bf16[272,256]{1,0:T(8,128)(2,1)S(1)} %get-tuple-element.29), channel_id=1, source_target_pairs={{128,0},{193,1},{129,64},{64,65},{0,128},{65,129},{1,192},{192,193... | collective-permute-start | bytes 417800 | tf_op jit(solution)/shard_map/ppermute | solution.py:293
  154.5 6.8 %collective-permute-start.28 = (bf16[272,256]{1,0:T(8,128)(2,1)S(1)}, bf16[272,256]{1,0:T(8,128)(2,1)S(1)}, u32[]{:S(2)}, u32[]{:S(2)}) collective-permute-start(bf16[272,256]{1,0:T(8,128)(2,1)S(1)} %get-tuple-element.30), channel_id=1, source_target_pairs={{129,0},{64,1},{0,64},{65,65},{1,128},{192,129},{128,192},{193,193... | collective-permute-start | bytes 417800 | tf_op jit(solution)/shard_map/ppermute | solution.py:293
  157.0 6.6 %collective-permute-start.29 = (bf16[272,256]{1,0:T(8,128)(2,1)S(1)}, bf16[272,256]{1,0:T(8,128)(2,1)S(1)}, u32[]{:S(2)}, u32[]{:S(2)}) collective-permute-start(bf16[272,256]{1,0:T(8,128)(2,1)S(1)} %get-tuple-element.31), channel_id=1, source_target_pairs={{0,0},{65,1},{1,64},{192,65},{128,128},{193,129},{129,192},{64,193... | collective-permute-start | bytes 417800 | tf_op jit(solution)/shard_map/ppermute | solution.py:293
  (8 other events, 45.0 us)
